TPU v7x, 32 devices: a whole 2x2x4 slice. The times are simulated.
32 devices in a mesh: parts: 2 (over y), node: 2 (over core), local: 8 (over z, x).
Axes of the slice: x: 2, y: 2, z: 4, core: 2. Of those that a mesh axis runs over, the one named last changes fastest.
Arguments:
- tokens: bfloat16 [2048, 7168], P(('parts', 'node', 'local')), parts along dimension 0, may hold values from -6 to 6
- experts: int32 [2048, 1], P(('parts', 'node', 'local')), parts along dimension 0, may hold values from 0 to 11; in each aligned block of 64 rows (0 to 63, 64 to 127, ...) at most 6 rows name the same one
- replicas: int32 [2048, 1], P(('parts', 'node', 'local')), parts along dimension 0, may hold values from 0 to 1
- gates: float32 [2048, 1], P(('parts', 'node', 'local')), parts along dimension 0, may hold values from 0.2 to 1
- placement: int32 [12, 2], replicated, may hold values from 0 to 15, as said below
- gate_weight: bfloat16 [16, 7168, 2048], P(('node', 'local')), may hold values from -0.0625 to 0.0625
- up_weight: bfloat16 [16, 7168, 2048], P(('node', 'local')), may hold values from -0.0625 to 0.0625
- down_weight: bfloat16 [16, 2048, 7168], P(('node', 'local')), may hold values from -0.125 to 0.125
Outputs:
- mixed: bfloat16 [2048, 7168], P(('parts', 'node', 'local')), parts along dimension 0
There are 2 independent parts, one for each index of `parts`. A program takes and returns all parts, laid end to end along the dimension named above; an argument that names none is the same for every part. Nothing has to cross between parts.
Inputs may be any that keep to these rules, and one draw needn't show every extreme that they name: `placement`: every copy 0 to 15 appears in the table; column 0 names 12 different copies, and column 1 names, for 4 experts, a further copy of their own, for the others the copy of column 0. `experts`: among the 64 tokens of one block no expert is picked more than 6 times, and some block picks some expert exactly 6 times.
All inputs are finite; a program needn't handle non-finite values.
Results may differ from a plain program's by a relative error of at most 0.0057.
Values may be sent and summed in bfloat16 or wider, within the bound.
No kernel may reach another device: no remote copies, remote signals or barrier semaphores. Data moves between devices by JAX's collectives and lax.ppermute only.
A program may use at most 192 MiB of HBM per device.

v0:
```python
import jax
import jax.numpy as jnp
from jax import lax
from jax.sharding import PartitionSpec as P

FF = 2048
CAP = 6


def route_tables(experts, replicas, gates, placement, slot_count, capacity):
    expert_hit = (
        experts[:, :, None] == jnp.arange(placement.shape[0], dtype=jnp.int32)[None, None, :]
    )
    replica_hit = (
        replicas[:, :, None] == jnp.arange(placement.shape[1], dtype=jnp.int32)[None, None, :]
    )
    joined = expert_hit[:, :, :, None] & replica_hit[:, :, None, :]
    slot_ids = jnp.sum(jnp.where(joined, placement[None, None, :, :], 0), axis=(2, 3))
    flat_slots = slot_ids.reshape(-1)
    slot_hit = (flat_slots[:, None] == jnp.arange(slot_count, dtype=jnp.int32)[None, :]).astype(
        jnp.int32
    )
    before = jnp.cumsum(slot_hit, axis=0) - slot_hit
    rank = jnp.sum(slot_hit * before, axis=1)
    position = (flat_slots * capacity + rank).reshape(slot_ids.shape)
    grid = position[:, :, None] == jnp.arange(slot_count * capacity, dtype=jnp.int32)[None, None, :]
    scatter = jnp.any(grid, axis=1).T
    zero_gate = jnp.zeros_like(gates)[:, :, None]
    combine = jnp.sum(jnp.where(grid, gates[:, :, None], zero_gate), axis=1)
    return (scatter, combine)


def per_device(tokens, experts, replicas, gates, placement, gate_weight, up_weight, down_weight):
    tok_rows, model_width = tokens.shape
    hidden_dev = gate_weight.shape[2]
    group_size = FF // hidden_dev
    devices_all = lax.axis_size(("node", "local"))
    slot_count = devices_all // group_size
    capacity = CAP
    scatter, combine = route_tables(experts, replicas, gates, placement, slot_count, capacity)
    outgoing = jnp.dot(
        scatter.astype(jnp.bfloat16), tokens, preferred_element_type=jnp.float32
    ).astype(jnp.bfloat16)
    outgoing = outgoing.reshape(slot_count, capacity, model_width)
    sending = jnp.repeat(outgoing, group_size, axis=0)
    arrived = lax.all_to_all(sending, ("node", "local"), split_axis=0, concat_axis=0, tiled=True)
    row_block = arrived.reshape(-1, model_width)
    gate_val = jnp.dot(row_block, gate_weight[0], preferred_element_type=jnp.float32)
    up_val = jnp.dot(row_block, up_weight[0], preferred_element_type=jnp.float32)
    hidden = (jax.nn.silu(gate_val) * up_val).astype(jnp.bfloat16)
    partial_value = (
        jnp.dot(hidden, down_weight[0], preferred_element_type=jnp.float32)
        .astype(jnp.bfloat16)
        .reshape(arrived.shape)
    )
    returned = lax.all_to_all(
        partial_value, ("node", "local"), split_axis=0, concat_axis=0, tiled=True
    )
    summed = jnp.sum(
        returned.reshape(slot_count, group_size, capacity, model_width).astype(jnp.float32), axis=1
    )
    mixed = jnp.dot(
        combine,
        summed.reshape(slot_count * capacity, model_width),
        precision=lax.Precision.HIGHEST,
        preferred_element_type=jnp.float32,
    )
    return mixed.astype(jnp.bfloat16)


def solution(mesh):
    in_specs = (
        P(("parts", "node", "local"), None),
        P(("parts", "node", "local"), None),
        P(("parts", "node", "local"), None),
        P(("parts", "node", "local"), None),
        P(),
        P(("node", "local"), None, None),
        P(("node", "local"), None, None),
        P(("node", "local"), None, None),
    )
    out_specs = P(("parts", "node", "local"), None)
    return jax.shard_map(
        per_device, mesh=mesh, in_specs=in_specs, out_specs=out_specs, check_vma=False
    )
```

profile of v0, /device:TPU:0, one launch (start us, length us, event | category | flops | bytes accessed | tf_op | source)
XLA Modules:
  0.0 145.8 jit_solution(15907246924060210189)
XLA Ops:
  0.0 0.0 copy-start
  0.0 0.8 copy.11
  0.9 0.7 iota_compare_fusion.3
  1.5 0.7 iota_compare_fusion.4
  2.2 0.1 fusion.25
  2.3 0.1 fusion.23
  2.3 0.1 reduce_window_sum.11
  2.4 0.2 select_reduce_fusion
  2.6 0.0 copy-done
  2.6 1.7 %convolution_convert_fusion = bf16[96,7168]{1,0:T(8,128)(2,1)} fusion(bf16[64,7168]{1,0:T(8,128)(2,1)S(1)} %copy-done, s32[64]{0:T(128)S(1)} %multiply_add_fusion), kind=kOutput, calls=%fused_computation.6 | convolution fusion | flops 88774656 | bytes 2294016 | tf_op jit(solution)/shard_map/dot_general | solution.py:41
  4.4 1.6 %reshape_broadcast_in_dim_reshape.3 = bf16[16,6,7168]{2,1,0:T(8,128)(2,1)S(1)} reshape(bf16[96,7168]{1,0:T(8,128)(2,1)} %convolution_convert_fusion) | data formatting | bytes 2752512 | tf_op jit(solution)/shard_map/reshape;broadcast_in_dim;reshape | solution.py:45
  6.0 51.3 %all_to_all.10 = bf16[16,6,7168]{2,1,0:T(8,128)(2,1)} all-to-all(bf16[16,6,7168]{2,1,0:T(8,128)(2,1)S(1)} %reshape_broadcast_in_dim_reshape.3), channel_id=1, replica_groups=mesh['parts'=2,'node'=2,'local'=8] {'node','local'}, dimensions={0} | all-to-all | bytes 2752512 | tf_op jit(solution)/shard_map/all_to_all | solution.py:46
  57.3 1.7 %reshape.175 = bf16[96,7168]{1,0:T(8,128)(2,1)S(1)} reshape(bf16[16,6,7168]{2,1,0:T(8,128)(2,1)} %all_to_all.10) | data formatting | bytes 2752512 | tf_op jit(solution)/shard_map/reshape | solution.py:47
  59.0 11.8 %fusion.4 = f32[96,2048]{1,0:T(8,128)S(1)} fusion(bf16[96,7168]{1,0:T(8,128)(2,1)S(1)} %reshape.175, bf16[1,7168,2048]{2,1,0:T(8,128)(2,1)} %param.13), kind=kOutput, calls=%fused_computation.4 | convolution fusion | flops 2818572288 | bytes 31522816 | tf_op jit(solution)/shard_map/dot_general | solution.py:48
  70.9 21.8 %fusion.6 = bf16[96,7168]{1,0:T(8,128)(2,1)} fusion(bf16[1,2048,7168]{2,1,0:T(8,128)(2,1)} %param.15, bf16[96,7168]{1,0:T(8,128)(2,1)S(1)} %reshape.175, bf16[1,7168,2048]{2,1,0:T(8,128)(2,1)} %param.14, f32[96,2048]{1,0:T(8,128)S(1)} %fusion.4), kind=kOutput, calls=%fused_computation.7 | convolution fusion | flops 5639012352 | bytes 62259200 | tf_op jit(solution)/shard_map/dot_general | solution.py:52
  92.7 2.6 %reshape.176 = bf16[16,6,7168]{2,1,0:T(8,128)(2,1)} reshape(bf16[96,7168]{1,0:T(8,128)(2,1)} %fusion.6) | data formatting | bytes 2752512 | tf_op jit(solution)/shard_map/reshape | solution.py:54
  95.3 0.0 copy-start.2
  95.3 3.8 %all-to-all-start.1 = ((bf16[16,6,7168]{2,1,0:T(8,128)(2,1)}), bf16[16,6,7168]{2,1,0:T(8,128)(2,1)S(1)}, u32[]{:S(2)}, u32[]{:S(2)}) async-start(bf16[16,6,7168]{2,1,0:T(8,128)(2,1)} %reshape.176), calls=%async_computation.1 | async-start | bytes 3670016 | tf_op jit(solution)/shard_map/all_to_all | solution.py:56
  99.1 0.0 copy-done.2
  99.2 0.2 compare_select_fusion
  99.4 42.0 %all-to-all-done.1 = bf16[16,6,7168]{2,1,0:T(8,128)(2,1)S(1)} async-done(((bf16[16,6,7168]{2,1,0:T(8,128)(2,1)}), bf16[16,6,7168]{2,1,0:T(8,128)(2,1)S(1)}, u32[]{:S(2)}, u32[]{:S(2)}) %all-to-all-start.1) | async-done | bytes 1376288 | tf_op jit(solution)/shard_map/all_to_all | solution.py:56
  141.4 1.4 reshape.177
  142.7 3.1 %convolution_convert_fusion.1 = bf16[64,7168]{1,0:T(8,128)(2,1)} fusion(f32[64,96]{1,0:T(8,128)S(1)} %bitcast.26, bf16[96,7168]{1,0:T(8,128)(2,1)} %reshape.177), kind=kOutput, calls=%fused_computation.8 | convolution fusion | flops 528941056 | bytes 2318336 | tf_op jit(solution)/shard_map/dot_general | solution.py:62
  145.8 0.0 copy-done.1
  (2 shorter events, 0.0 us)
Async XLA Ops:
  0.0 2.6 %copy-start = (bf16[64,7168]{1,0:T(8,128)(2,1)S(1)}, bf16[64,7168]{1,0:T(8,128)(2,1)}, u32[]{:S(2)}) copy-start(bf16[64,7168]{1,0:T(8,128)(2,1)} %param.8) | copy-start | bytes 2752516
  95.3 3.9 %copy-start.2 = (f32[64,1]{0,1:T(1,128)S(1)}, f32[64,1]{0,1:T(1,128)}, u32[]{:S(2)}) copy-start(f32[64,1]{0,1:T(1,128)} %param.11) | copy-start | bytes 772
  95.3 46.1 %all-to-all-start.1 = ((bf16[16,6,7168]{2,1,0:T(8,128)(2,1)}), bf16[16,6,7168]{2,1,0:T(8,128)(2,1)S(1)}, u32[]{:S(2)}, u32[]{:S(2)}) async-start(bf16[16,6,7168]{2,1,0:T(8,128)(2,1)} %reshape.176), calls=%async_computation.1 | async-start | bytes 3670016 | tf_op jit(solution)/shard_map/all_to_all | solution.py:56
  141.4 4.5 %copy-start.1 = (bf16[64,7168]{1,0:T(8,128)(2,1)S(1)}, bf16[64,7168]{1,0:T(8,128)(2,1)}, u32[]{:S(2)}) copy-start(bf16[64,7168]{1,0:T(8,128)(2,1)} %param.8) | copy-start | bytes 2752516
where the time goes:
time: 146 us
  blocking collectives  51.3 us (35%)
  waiting for transfers between devices  42 us (29%)
  matrix products  38.5 us (26%)
  local copies, waits for them, and re-layouts  8.16 us (6%)
  starting transfers between devices  3.84 us (3%)
  other arithmetic  1.97 us (1%)
    all_to_all x1, blocking collectives, per_device(): lax.all_to_all(sending, ('node', 'local'), split_axis=0, concat_axis=0, t...  51.3 us
    all_to_all x1, waiting for transfers between devices, per_device(): lax.all_to_all(partial_value, ('node', 'local'), split_axis=0, concat_axi...  42 us
    dot_general x1, matrix products, per_device(): jnp.dot(hidden, down_weight[0], preferred_element_type=jnp.float32)  21.8 us
    dot_general x1, matrix products, per_device(): jnp.dot(row_block, gate_weight[0], preferred_element_type=jnp.float32)  11.8 us
    all_to_all x1, starting transfers between devices, per_device(): lax.all_to_all(partial_value, ('node', 'local'), split_axis=0, concat_axi...  3.84 us
    dot_general x1, matrix products, per_device(): jnp.dot(combine, summed.reshape(slot_count * capacity, model_width), prec...  3.12 us
  transfers between devices with their start and end apart: 1, of which 1 were waited for; matrix products, arithmetic and copies ran while one was open for 0% of the time, Pallas kernels for 0%

commit v1 on v0

--- a/solution.py
+++ b/solution.py
@@ -1,10 +1,21 @@
+import functools
+
 import jax
 import jax.numpy as jnp
+import numpy as np
 from jax import lax
+from jax.experimental import pallas as pl
+from jax.experimental.pallas import tpu as pltpu
 from jax.sharding import PartitionSpec as P
 
 FF = 2048
 CAP = 6
+FOLD = 4
+STEP = 256
+HOPS = (1, 2, 4, 6, 5, 7, 3)
+DISPATCH = (1024, 768)
+RETURN = (512, 1280)
+VMEM_BYTES = 56 * 1024 * 1024
 
 
 def route_tables(experts, replicas, gates, placement, slot_count, capacity):
@@ -30,8 +41,10 @@
     return (scatter, combine)
 
 
-def per_device(tokens, experts, replicas, gates, placement, gate_weight, up_weight, down_weight):
-    tok_rows, model_width = tokens.shape
+def per_device_general(
+    tokens, experts, replicas, gates, placement, gate_weight, up_weight, down_weight
+):
+    model_width = tokens.shape[1]
     hidden_dev = gate_weight.shape[2]
     group_size = FF // hidden_dev
     devices_all = lax.axis_size(("node", "local"))
@@ -68,6 +81,401 @@
     return mixed.astype(jnp.bfloat16)
 
 
+def params(**kw):
+    return pltpu.CompilerParams(vmem_limit_bytes=VMEM_BYTES, **kw)
+
+
+def whole(shape):
+    return pl.BlockSpec(shape, lambda *_: (0,) * len(shape))
+
+
+def cost(flops, size):
+    return pl.CostEstimate(flops=int(flops), bytes_accessed=int(size), transcendentals=0)
+
+
+def fold_order(groups):
+    g, q, c = np.meshgrid(np.arange(groups), np.arange(FOLD), np.arange(CAP), indexing="ij")
+    order = np.zeros(groups * FOLD * CAP, np.int64)
+    order[(q * groups * CAP + g * CAP + c).ravel()] = (g * FOLD * CAP + q * CAP + c).ravel()
+    return order
+
+
+def dispatch_kernel(n_local, widths, place_ref, who_ref, pick_ref, own_ref, mate_ref, *outs):
+    base_ref, blocks = outs[0], outs[1:]
+    tok = own_ref.shape[0]
+    both = 2 * tok
+    node, local = who_ref[0], who_ref[1]
+    pick = pick_ref[...]
+    slot = jnp.zeros((1, both), jnp.int32)
+    for e in range(place_ref.shape[0]):
+        for r in range(place_ref.shape[1]):
+            slot = jnp.where(pick == e * place_ref.shape[1] + r, place_ref[e, r], slot)
+    slots = 2 * n_local
+    hit = lax.broadcasted_iota(jnp.int32, (slots, both), 0) == slot
+    early = lax.broadcasted_iota(jnp.int32, (both, both), 0)
+    late = lax.broadcasted_iota(jnp.int32, (both, both), 1)
+    same_block = (early >= tok) == (late >= tok)
+    earlier = ((early < late) & same_block).astype(jnp.bfloat16)
+    before = jnp.dot(hit.astype(jnp.bfloat16), earlier, preferred_element_type=jnp.float32)
+    rank = jnp.sum(jnp.where(hit, before, 0.0), axis=0, keepdims=True).astype(jnp.int32)
+    place_of = slot - node * n_local
+    here = (place_of >= 0) & (place_of < n_local)
+    hop = place_of ^ local
+    second = (lax.broadcasted_iota(jnp.int32, (1, both), 1) >= tok).astype(jnp.int32)
+    base = jnp.where(here, (hop * 2 + second) * (FOLD * CAP) + rank, -FOLD * CAP)
+    base_ref[...] = base
+    rows = slots * FOLD * CAP
+    row = lax.broadcasted_iota(jnp.int32, (rows, both), 0)
+    select = jnp.concatenate(
+        [(row == base + q * CAP).astype(jnp.bfloat16) for q in range(FOLD)], axis=1
+    )
+    size = 2 * FOLD * CAP
+    start = 0
+    for piece, width in enumerate(widths):
+        folded = jnp.concatenate(
+            [
+                ref[:, start + q * width : start + (q + 1) * width]
+                for q in range(FOLD)
+                for ref in (own_ref, mate_ref)
+            ],
+            axis=0,
+        )
+        value = jnp.dot(select, folded, preferred_element_type=jnp.float32).astype(jnp.bfloat16)
+        for hop_id in range(n_local):
+            blocks[piece * n_local + hop_id][...] = value[hop_id * size : (hop_id + 1) * size]
+        start += FOLD * width
+
+
+def dispatch(place, who, pick, own, mate, n_local):
+    tok, model = own.shape
+    size = 2 * FOLD * CAP
+    out_shape = [jax.ShapeDtypeStruct((1, 2 * tok), jnp.int32)] + [
+        jax.ShapeDtypeStruct((size, width), jnp.bfloat16)
+        for width in DISPATCH
+        for _ in range(n_local)
+    ]
+    smem = pl.BlockSpec(memory_space=pltpu.SMEM)
+    vmem = pl.BlockSpec(memory_space=pltpu.VMEM)
+    outs = pl.pallas_call(
+        functools.partial(dispatch_kernel, n_local, DISPATCH),
+        out_shape=out_shape,
+        in_specs=[smem, smem, vmem, vmem, vmem],
+        out_specs=[vmem] * len(out_shape),
+        compiler_params=params(),
+        cost_estimate=cost(2e9, 6e6),
+        name="dispatch",
+    )(place, who, pick, own, mate)
+    pieces = [
+        outs[1 + i * n_local : 1 + (i + 1) * n_local] for i in range(len(DISPATCH))
+    ]
+    return outs[0], pieces
+
+
+def unfold(blocks, order_ref, x_ref, rows, width):
+    folded = jnp.concatenate([b[...] for b in blocks], axis=0)
+    value = jnp.dot(order_ref[...], folded, preferred_element_type=jnp.float32)
+    value = value.astype(jnp.bfloat16)
+    tiles = width // STEP
+    for q in range(FOLD):
+        for j in range(tiles):
+            x_ref[q * tiles + j] = value[
+                q * rows : (q + 1) * rows, j * STEP : (j + 1) * STEP
+            ]
+
+
+def refold(tiles_ref, order_ref, blocks, width):
+    tiles = width // STEP
+    value = jnp.concatenate(
+        [
+            jnp.concatenate([tiles_ref[q * tiles + j] for j in range(tiles)], axis=1)
+            for q in range(FOLD)
+        ],
+        axis=0,
+    )
+    folded = jnp.dot(order_ref[...], value, preferred_element_type=jnp.float32)
+    folded = folded.astype(jnp.bfloat16)
+    size = 2 * FOLD * CAP
+    for i, block in enumerate(blocks):
+        block[...] = folded[i * size : (i + 1) * size]
+
+
+def first_kernel(n_local, width, order_ref, *refs):
+    blocks = refs[:n_local]
+    wg_ref, wu_ref, accg_ref, accu_ref, x_ref = refs[n_local:]
+    i = pl.program_id(0)
+    rows = 2 * n_local * CAP
+
+    @pl.when(i == 0)
+    def _():
+        unfold(blocks, order_ref, x_ref, rows, width)
+        accg_ref[...] = jnp.zeros_like(accg_ref)
+        accu_ref[...] = jnp.zeros_like(accu_ref)
+
+    x = x_ref[i]
+    accg_ref[...] += jnp.dot(x, wg_ref[0], preferred_element_type=jnp.float32)
+    accu_ref[...] += jnp.dot(x, wu_ref[0], preferred_element_type=jnp.float32)
+
+
+def first_part(order, blocks, gate_weight, up_weight, start, width):
+    n_local = len(blocks)
+    rows = 2 * n_local * CAP
+    hidden = gate_weight.shape[2]
+    steps = FOLD * width // STEP
+    weight = pl.BlockSpec((1, STEP, hidden), lambda i: (0, start // STEP + i, 0))
+    acc = jax.ShapeDtypeStruct((rows, hidden), jnp.float32)
+    return pl.pallas_call(
+        functools.partial(first_kernel, n_local, width),
+        grid=(steps,),
+        out_shape=[acc, acc],
+        in_specs=[whole(order.shape)] + [whole(b.shape) for b in blocks] + [weight, weight],
+        out_specs=[whole(acc.shape)] * 2,
+        scratch_shapes=[pltpu.VMEM((steps, rows, STEP), jnp.bfloat16)],
+        compiler_params=params(),
+        cost_estimate=cost(
+            4 * rows * FOLD * width * hidden, 4 * FOLD * width * hidden
+        ),
+        name="first_part",
+    )(order, *blocks, gate_weight, up_weight)
+
+
+def middle_kernel(n_local, width, width_out, order_ref, back_ref, *refs):
+    blocks = refs[:n_local]
+    ing_ref, inu_ref, wg_ref, wu_ref, wd_ref = refs[n_local : n_local + 5]
+    hidden_ref = refs[n_local + 5]
+    outs = refs[n_local + 6 : 2 * n_local + 6]
+    x_ref, accg_ref, accu_ref, o_ref = refs[2 * n_local + 6 :]
+    i = pl.program_id(0)
+    rows = 2 * n_local * CAP
+    steps = FOLD * width // STEP
+    steps_out = FOLD * width_out // STEP
+
+    @pl.when(i == 0)
+    def _():
+        unfold(blocks, order_ref, x_ref, rows, width)
+        accg_ref[...] = ing_ref[...]
+        accu_ref[...] = inu_ref[...]
+
+    @pl.when(i < steps)
+    def _():
+        x = x_ref[i]
+        accg_ref[...] += jnp.dot(x, wg_ref[0], preferred_element_type=jnp.float32)
+        accu_ref[...] += jnp.dot(x, wu_ref[0], preferred_element_type=jnp.float32)
+
+    @pl.when(i == steps - 1)
+    def _():
+        gate_val = accg_ref[...]
+        hidden_ref[...] = (gate_val / (1.0 + jnp.exp(-gate_val)) * accu_ref[...]).astype(
+            jnp.bfloat16
+        )
+
+    @pl.when(i >= steps)
+    def _():
+        o_ref[i - steps] = jnp.dot(
+            hidden_ref[...], wd_ref[0], preferred_element_type=jnp.float32
+        ).astype(jnp.bfloat16)
+
+    @pl.when(i == steps + steps_out - 1)
+    def _():
+        refold(o_ref, back_ref, outs, width_out)
+
+
+def middle_part(
+    order, back, blocks, accs, gate_weight, up_weight, down_weight, start, width, width_out
+):
+    n_local = len(blocks)
+    rows = 2 * n_local * CAP
+    hidden = gate_weight.shape[2]
+    steps = FOLD * width // STEP
+    steps_out = FOLD * width_out // STEP
+    weight = pl.BlockSpec(
+        (1, STEP, hidden), lambda i: (0, start // STEP + jnp.minimum(i, steps - 1), 0)
+    )
+    down = pl.BlockSpec((1, hidden, STEP), lambda i: (0, 0, jnp.maximum(i - steps, 0)))
+    size = 2 * FOLD * CAP
+    out_shape = [jax.ShapeDtypeStruct((rows, hidden), jnp.bfloat16)] + [
+        jax.ShapeDtypeStruct((size, width_out), jnp.bfloat16) for _ in range(n_local)
+    ]
+    outs = pl.pallas_call(
+        functools.partial(middle_kernel, n_local, width, width_out),
+        grid=(steps + steps_out,),
+        out_shape=out_shape,
+        in_specs=[whole(order.shape), whole(back.shape)]
+        + [whole(b.shape) for b in blocks]
+        + [whole(a.shape) for a in accs]
+        + [weight, weight, down],
+        out_specs=[whole(o.shape) for o in out_shape],
+        scratch_shapes=[
+            pltpu.VMEM((steps, rows, STEP), jnp.bfloat16),
+            pltpu.VMEM((rows, hidden), jnp.float32),
+            pltpu.VMEM((rows, hidden), jnp.float32),
+            pltpu.VMEM((steps_out, rows, STEP), jnp.bfloat16),
+        ],
+        compiler_params=params(),
+        cost_estimate=cost(
+            2 * rows * FOLD * (2 * width + width_out) * hidden,
+            2 * FOLD * (2 * width + width_out) * hidden,
+        ),
+        name="middle_part",
+    )(order, back, *blocks, *accs, gate_weight, up_weight, down_weight)
+    return outs[0], outs[1:]
+
+
+def last_kernel(n_local, width, back_ref, hidden_ref, wd_ref, *refs):
+    outs, o_ref = refs[:n_local], refs[n_local]
+    i = pl.program_id(0)
+    o_ref[i] = jnp.dot(hidden_ref[...], wd_ref[0], preferred_element_type=jnp.float32).astype(
+        jnp.bfloat16
+    )
+
+    @pl.when(i == pl.num_programs(0) - 1)
+    def _():
+        refold(o_ref, back_ref, outs, width)
+
+
+def last_part(back, hidden, down_weight, start, width, n_local):
+    rows, inner = hidden.shape
+    steps = FOLD * width // STEP
+    size = 2 * FOLD * CAP
+    out_shape = [jax.ShapeDtypeStruct((size, width), jnp.bfloat16) for _ in range(n_local)]
+    return pl.pallas_call(
+        functools.partial(last_kernel, n_local, width),
+        grid=(steps,),
+        out_shape=out_shape,
+        in_specs=[
+            whole(back.shape),
+            whole(hidden.shape),
+            pl.BlockSpec((1, inner, STEP), lambda i: (0, 0, start // STEP + i)),
+        ],
+        out_specs=[whole(o.shape) for o in out_shape],
+        scratch_shapes=[pltpu.VMEM((steps, rows, STEP), jnp.bfloat16)],
+        compiler_params=params(),
+        cost_estimate=cost(
+            2 * rows * FOLD * width * inner, 2 * FOLD * width * inner
+        ),
+        name="last_part",
+    )(back, hidden, down_weight)
+
+
+def column(row):
+    n = row.shape[1]
+    eye = lax.broadcasted_iota(jnp.int32, (n, n), 0) == lax.broadcasted_iota(jnp.int32, (n, n), 1)
+    return jnp.sum(jnp.where(eye, row, jnp.zeros_like(row)), axis=1, keepdims=True)
+
+
+def pick_kernel(n_local, base_ref, *refs):
+    blocks = refs[:n_local]
+    own_ref, mate_ref = refs[n_local:]
+    tok = own_ref.shape[0]
+    width = blocks[0].shape[1]
+    base = column(base_ref[...])
+    folded = jnp.concatenate([b[...] for b in blocks], axis=0)
+    lane = lax.broadcasted_iota(jnp.int32, (base.shape[0], folded.shape[0]), 1)
+    for q in range(FOLD):
+        select = (lane == base + q * CAP).astype(jnp.bfloat16)
+        value = jnp.dot(select, folded, preferred_element_type=jnp.float32).astype(jnp.bfloat16)
+        own_ref[:, q * width : (q + 1) * width] = value[:tok]
+        mate_ref[:, q * width : (q + 1) * width] = value[tok:]
+
+
+def pick_rows(base, blocks):
+    n_local = len(blocks)
+    tok = base.shape[1] // 2
+    width = blocks[0].shape[1]
+    vmem = pl.BlockSpec(memory_space=pltpu.VMEM)
+    half = jax.ShapeDtypeStruct((tok, FOLD * width), jnp.bfloat16)
+    return pl.pallas_call(
+        functools.partial(pick_kernel, n_local),
+        out_shape=[half, half],
+        in_specs=[vmem] * (1 + n_local),
+        out_specs=[vmem] * 2,
+        compiler_params=params(),
+        cost_estimate=cost(8 * tok * width * 384 * 2, 6 * tok * FOLD * width),
+        name="pick_rows",
+    )(base, *blocks)
+
+
+def mix_kernel(count, gates_ref, *refs):
+    own, other, out_ref = refs[:count], refs[count : 2 * count], refs[2 * count]
+    gate = column(gates_ref[...])
+    start = 0
+    for a, b in zip(own, other):
+        width = a.shape[1]
+        total = a[...].astype(jnp.float32) + b[...].astype(jnp.float32)
+        out_ref[:, start : start + width] = (gate * total).astype(jnp.bfloat16)
+        start += width
+
+
+def mix(gates, own, other):
+    tok = own[0].shape[0]
+    model = sum(a.shape[1] for a in own)
+    vmem = pl.BlockSpec(memory_space=pltpu.VMEM)
+    return pl.pallas_call(
+        functools.partial(mix_kernel, len(own)),
+        out_shape=jax.ShapeDtypeStruct((tok, model), jnp.bfloat16),
+        in_specs=[vmem] * (1 + 2 * len(own)),
+        out_specs=vmem,
+        compiler_params=params(),
+        cost_estimate=cost(3 * tok * model, 6 * tok * model),
+        name="mix",
+    )(gates, *own, *other)
+
+
+def swap_hops(blocks):
+    n_local = len(blocks)
+    out = list(blocks)
+    for hop in HOPS:
+        if hop < n_local:
+            out[hop] = lax.ppermute(
+                blocks[hop], "local", [(i, i ^ hop) for i in range(n_local)]
+            )
+    return out
+
+
+def swap_mate(value):
+    return lax.ppermute(value, "node", [(0, 1), (1, 0)])
+
+
+def per_device_folded(
+    tokens, experts, replicas, gates, placement, gate_weight, up_weight, down_weight
+):
+    tok = tokens.shape[0]
+    n_local = lax.axis_size("local")
+    pick = (experts * placement.shape[1] + replicas).reshape(1, tok)
+    mate_tokens = swap_mate(tokens)
+    picks = jnp.concatenate([pick, swap_mate(pick)], axis=1)
+    who = jnp.stack([lax.axis_index("node"), lax.axis_index("local")]).astype(jnp.int32)
+    order = fold_order(2 * n_local)
+    size = order.shape[0]
+    forward = np.zeros((size, size), np.float32)
+    forward[np.arange(size), order] = 1.0
+    unfold_order = jnp.asarray(forward, jnp.bfloat16)
+    refold_order = jnp.asarray(forward.T, jnp.bfloat16)
+
+    base, pieces = dispatch(placement, who, picks, tokens, mate_tokens, n_local)
+    arrived = [swap_hops(piece) for piece in pieces]
+    accs = first_part(unfold_order, arrived[0], gate_weight, up_weight, 0, DISPATCH[0])
+    hidden, back_first = middle_part(
+        unfold_order,
+        refold_order,
+        arrived[1],
+        accs,
+        gate_weight,
+        up_weight,
+        down_weight,
+        FOLD * DISPATCH[0],
+        DISPATCH[1],
+        RETURN[0],
+    )
+    returned = [swap_hops(back_first)]
+    back_second = last_part(
+        refold_order, hidden, down_weight, FOLD * RETURN[0], RETURN[1], n_local
+    )
+    returned.append(swap_hops(back_second))
+    picked = [pick_rows(base, blocks) for blocks in returned]
+    other = [swap_mate(pair[1]) for pair in picked]
+    return mix(gates.reshape(1, tok), [pair[0] for pair in picked], other)
+
+
 def solution(mesh):
     in_specs = (
         P(("parts", "node", "local"), None),
@@ -80,6 +488,16 @@
         P(("node", "local"), None, None),
     )
     out_specs = P(("parts", "node", "local"), None)
+
+    def per_device(*args):
+        folded = (
+            mesh.shape["node"] == 2
+            and mesh.shape["local"] == 8
+            and args[5].shape[2] == FF
+            and args[0].shape[1] == FOLD * sum(DISPATCH)
+        )
+        return (per_device_folded if folded else per_device_general)(*args)
+
     return jax.shard_map(
         per_device, mesh=mesh, in_specs=in_specs, out_specs=out_specs, check_vma=False
     )

time: 146 us -> 164 us (1.12)
  Pallas kernels: 0 us -> 74 us
  blocking collectives: 51.3 us -> 0 us
  starting transfers between devices: 3.84 us -> 51.3 us
  matrix products: 38.5 us -> 0 us
  waiting for transfers between devices: 42 us -> 29.8 us
  local copies, waits for them, and re-layouts: 8.16 us -> 5.19 us
    pallas_call x0 -> x7, Pallas kernels: none -> 74 us  [the longest x1 23.8 us: middle_part(): pl.pallas_call(functools.partial(middle_kernel, n_local, width, width_out...]
    all_to_all x1 -> x0, blocking collectives: 51.3 us -> none  [per_device(): lax.all_to_all(sending, ('node', 'local'), split_axis=0, concat_axis=0, t...]
    ppermute x0 -> x32, starting transfers between devices: none -> 51.3 us  [the longest x28 50.7 us: swap_hops(): lax.ppermute(blocks[hop], 'local', [(i, i ^ hop) for i in range(n_local)])]
    all_to_all x1 -> x0, waiting for transfers between devices: 42 us -> none  [per_device(): lax.all_to_all(partial_value, ('node', 'local'), split_axis=0, concat_axi...]
    dot_general x4 -> x0, matrix products: 38.5 us -> none  [the longest x1 21.8 us: per_device(): jnp.dot(hidden, down_weight[0], preferred_element_type=jnp.float32)]
    ppermute x0 -> x32, waiting for transfers between devices: none -> 29.8 us  [the longest x28 28.1 us: swap_hops(): lax.ppermute(blocks[hop], 'local', [(i, i ^ hop) for i in range(n_local)])]
    reshape x3 -> x0, local copies, waits for them, and re-layouts: 5.68 us -> none  [the longest x1 2.6 us: per_device(): partial_value = jnp.dot(hidden, down_weight[0], preferred_element_type=jn...]
    unnamed x7 -> x77, local copies, waits for them, and re-layouts: 0.86 us -> 5.19 us
  transfers between devices with their start and end apart: 1 -> 32, of which waited for: 1 -> 11; matrix products, arithmetic and copies ran while one was open for 0% -> 2% of each run, Pallas kernels for 0% -> 14%
where the time goes in v1:
time: 164 us; the launch traced here: 163 us
  Pallas kernels  74 us (45%)
  starting transfers between devices  51.3 us (31%)
  waiting for transfers between devices  29.8 us (18%)
  local copies, waits for them, and re-layouts  5.19 us (3%)
  other arithmetic  1.92 us (1%)
    ppermute x28, starting transfers between devices, swap_hops(): lax.ppermute(blocks[hop], 'local', [(i, i ^ hop) for i in range(n_local)])  50.7 us
    ppermute x28, waiting for transfers between devices, swap_hops(): lax.ppermute(blocks[hop], 'local', [(i, i ^ hop) for i in range(n_local)])  28.1 us
    pallas_call x1, Pallas kernels, middle_part(): pl.pallas_call(functools.partial(middle_kernel, n_local, width, width_out...  23.8 us
    pallas_call x1, Pallas kernels, first_part(): pl.pallas_call(functools.partial(first_kernel, n_local, width), grid=(ste...  19.9 us
    pallas_call x1, Pallas kernels, last_part(): pl.pallas_call(functools.partial(last_kernel, n_local, width), grid=(step...  18.5 us
    pallas_call x2, Pallas kernels, pick_rows(): pl.pallas_call(functools.partial(pick_kernel, n_local), out_shape=[half,...  5.54 us
    unnamed x77, local copies, waits for them, and re-layouts  5.19 us
  transfers between devices with their start and end apart: 32, of which 11 were waited for; matrix products, arithmetic and copies ran while one was open for 2% of the time, Pallas kernels for 14%

profile of v1, /device:TPU:0, one launch (start us, length us, event | category | flops | bytes accessed | tf_op | source)
XLA Modules:
  0.0 162.5 jit_solution(16373350287820329374)
XLA Ops:
  4.7 3.3 %dispatch.1 = (s32[1,128]{1,0:T(1,128)}, bf16[48,1024]{1,0:T(8,128)(2,1)}, bf16[48,1024]{1,0:T(8,128)(2,1)}, bf16[48,1024]{1,0:T(8,128)(2,1)}, bf16[48,1024]{1,0...) custom-call(s32[12,2]{1,0:T(8,128)} %copy.11.place_ref, ...), custom_call_target="tpu_custom_call" | custom-call | flops 2000000000 | bytes 6000000 | tf_op jit(solution)/shard_map/dispatch/pallas_call | solution.py:159
  8.0 2.9 %collective-permute-start.9 = (bf16[48,1024]{1,0:T(8,128)(2,1)}, bf16[48,1024]{1,0:T(8,128)(2,1)S(1)}, u32[]{:S(2)}, u32[]{:S(2)}) collective-permute-start(bf16[48,1024]{1,0:T(8,128)(2,1)} %get-tuple-element.55), channel_id=1, source_target_pairs={{0,1},{1,0},{2,3},{3,2},{4,5},{5,4},{6,7},{7,6},{8,9},{9,8},{10,11... | collective-permute-start | bytes 294920 | tf_op jit(solution)/shard_map/ppermute | solution.py:428
  13.0 3.0 %collective-permute-start.11 = (bf16[48,1024]{1,0:T(8,128)(2,1)}, bf16[48,1024]{1,0:T(8,128)(2,1)S(1)}, u32[]{:S(2)}, u32[]{:S(2)}) collective-permute-start(bf16[48,1024]{1,0:T(8,128)(2,1)} %get-tuple-element.57), channel_id=1, source_target_pairs={{0,3},{1,2},{2,1},{3,0},{4,7},{5,6},{6,5},{7,4},{8,11},{9,10},{10,... | collective-permute-start | bytes 294920 | tf_op jit(solution)/shard_map/ppermute | solution.py:428
  16.0 2.1 %collective-permute-done.2.refs_1_ = bf16[48,768]{1,0:T(8,128)(2,1)S(1)} collective-permute-done((bf16[48,768]{1,0:T(8,128)(2,1)}, bf16[48,768]{1,0:T(8,128)(2,1)S(1)}, u32[]{:S(2)}, u32[]{:S(2)}) %collective-permute-start.2) | collective-permute-done | bytes 73760 | tf_op jit(solution)/shard_map/ppermute | solution.py:428
  18.1 2.6 %collective-permute-start.12 = (bf16[48,1024]{1,0:T(8,128)(2,1)}, bf16[48,1024]{1,0:T(8,128)(2,1)S(1)}, u32[]{:S(2)}, u32[]{:S(2)}) collective-permute-start(bf16[48,1024]{1,0:T(8,128)(2,1)} %get-tuple-element.58), channel_id=1, source_target_pairs={{0,4},{1,5},{2,6},{3,7},{4,0},{5,1},{6,2},{7,3},{8,12},{9,13},{10,... | collective-permute-start | bytes 294920 | tf_op jit(solution)/shard_map/ppermute | solution.py:428
  21.2 2.2 %collective-permute-start.14 = (bf16[48,1024]{1,0:T(8,128)(2,1)}, bf16[48,1024]{1,0:T(8,128)(2,1)S(1)}, u32[]{:S(2)}, u32[]{:S(2)}) collective-permute-start(bf16[48,1024]{1,0:T(8,128)(2,1)} %get-tuple-element.60), channel_id=1, source_target_pairs={{0,6},{1,7},{2,4},{3,5},{4,2},{5,3},{6,0},{7,1},{8,14},{9,15},{10,... | collective-permute-start | bytes 294920 | tf_op jit(solution)/shard_map/ppermute | solution.py:428
  23.4 2.4 %collective-permute-start.15 = (bf16[48,1024]{1,0:T(8,128)(2,1)}, bf16[48,1024]{1,0:T(8,128)(2,1)S(1)}, u32[]{:S(2)}, u32[]{:S(2)}) collective-permute-start(bf16[48,1024]{1,0:T(8,128)(2,1)} %get-tuple-element.61), channel_id=1, source_target_pairs={{0,7},{1,6},{2,5},{3,4},{4,3},{5,2},{6,1},{7,0},{8,15},{9,14},{10,... | collective-permute-start | bytes 294920 | tf_op jit(solution)/shard_map/ppermute | solution.py:428
  25.8 7.1 %collective-permute-done.12.refs_4_ = bf16[48,1024]{1,0:T(8,128)(2,1)S(1)} collective-permute-done((bf16[48,1024]{1,0:T(8,128)(2,1)}, bf16[48,1024]{1,0:T(8,128)(2,1)S(1)}, u32[]{:S(2)}, u32[]{:S(2)}) %collective-permute-start.12) | collective-permute-done | bytes 98336 | tf_op jit(solution)/shard_map/ppermute | solution.py:428
  34.6 3.5 %collective-permute-start.7 = (bf16[48,768]{1,0:T(8,128)(2,1)}, bf16[48,768]{1,0:T(8,128)(2,1)S(1)}, u32[]{:S(2)}, u32[]{:S(2)}) collective-permute-start(bf16[48,768]{1,0:T(8,128)(2,1)} %get-tuple-element.52), channel_id=1, source_target_pairs={{0,6},{1,7},{2,4},{3,5},{4,2},{5,3},{6,0},{7,1},{8,14},{9,15},{10,... | collective-permute-start | bytes 221192 | tf_op jit(solution)/shard_map/ppermute | solution.py:428
  38.1 2.5 %collective-permute-start.8 = (bf16[48,768]{1,0:T(8,128)(2,1)}, bf16[48,768]{1,0:T(8,128)(2,1)S(1)}, u32[]{:S(2)}, u32[]{:S(2)}) collective-permute-start(bf16[48,768]{1,0:T(8,128)(2,1)} %get-tuple-element.53), channel_id=1, source_target_pairs={{0,7},{1,6},{2,5},{3,4},{4,3},{5,2},{6,1},{7,0},{8,15},{9,14},{10,... | collective-permute-start | bytes 221192 | tf_op jit(solution)/shard_map/ppermute | solution.py:428
  40.6 19.9 %first_part.1 = (f32[96,2048]{1,0:T(8,128)}, f32[96,2048]{1,0:T(8,128)}) custom-call(bf16[384,384]{1,0:T(8,128)(2,1)} %constant.15.clone.order_ref, bf16[48,1024]{1,0:T(8,128)(2,1)} %get-tuple-element.54.refs_0_, bf16[48,1024]{1,0:T(8,128)(2,1)} %copy-done.2, bf16[48,1024]{1,0:T(8,128)(2,1)} %copy-done.3, bf16[48,1024]{1,0:T(8,128)(2,1)} %copy-done.4, ...), custom_call_target="tpu_custom_call" | custom-call | flops 3221225472 | bytes 33554432 | tf_op jit(solution)/shard_map/first_part/pallas_call | solution.py:226
  61.3 23.8 %middle_part.1 = (bf16[96,2048]{1,0:T(8,128)(2,1)}, bf16[48,512]{1,0:T(8,128)(2,1)}, bf16[48,512]{1,0:T(8,128)(2,1)}, bf16[48,512]{1,0:T(8,128)(2,1)}, bf16[48,5...) custom-call(bf16[384,384]{1,0:T(8,128)(2,1)} %constant.15.clone.orde, ...), custom_call_target="tpu_custom_call" | custom-call | flops 3221225472 | bytes 33554432 | tf_op jit(solution)/shard_map/middle_part/pallas_call | solution.py:298
  85.2 18.5 %last_part.1 = (bf16[48,1280]{1,0:T(8,128)(2,1)}, bf16[48,1280]{1,0:T(8,128)(2,1)}, bf16[48,1280]{1,0:T(8,128)(2,1)}, bf16[48,1280]{1,0:T(8,128)(2,1)}, bf16[48,...) custom-call(bf16[384,384]{1,0:T(8,128)(2,1)} %constant.16.clone.back_ref, ...), custom_call_target="tpu_custom_call" | custom-call | flops 2013265920 | bytes 20971520 | tf_op jit(solution)/shard_map/last_part/pallas_call | solution.py:340
  103.7 7.5 %collective-permute-start.24 = (bf16[48,1280]{1,0:T(8,128)(2,1)}, bf16[48,1280]{1,0:T(8,128)(2,1)S(1)}, u32[]{:S(2)}, u32[]{:S(2)}) collective-permute-start(bf16[48,1280]{1,0:T(8,128)(2,1)} %get-tuple-element.76), channel_id=1, source_target_pairs={{0,2},{1,3},{2,0},{3,1},{4,6},{5,7},{6,4},{7,5},{8,10},{9,11},{10,... | collective-permute-start | bytes 368648 | tf_op jit(solution)/shard_map/ppermute | solution.py:428
  111.3 3.0 %collective-permute-start.26 = (bf16[48,1280]{1,0:T(8,128)(2,1)}, bf16[48,1280]{1,0:T(8,128)(2,1)S(1)}, u32[]{:S(2)}, u32[]{:S(2)}) collective-permute-start(bf16[48,1280]{1,0:T(8,128)(2,1)} %get-tuple-element.78), channel_id=1, source_target_pairs={{0,4},{1,5},{2,6},{3,7},{4,0},{5,1},{6,2},{7,3},{8,12},{9,13},{10,... | collective-permute-start | bytes 368648 | tf_op jit(solution)/shard_map/ppermute | solution.py:428
  119.8 8.4 %collective-permute-done.26.refs_4_ = bf16[48,1280]{1,0:T(8,128)(2,1)S(1)} collective-permute-done((bf16[48,1280]{1,0:T(8,128)(2,1)}, bf16[48,1280]{1,0:T(8,128)(2,1)S(1)}, u32[]{:S(2)}, u32[]{:S(2)}) %collective-permute-start.26) | collective-permute-done | bytes 122912 | tf_op jit(solution)/shard_map/ppermute | solution.py:428
  128.2 3.5 %collective-permute-done.27.refs_5_ = bf16[48,1280]{1,0:T(8,128)(2,1)S(1)} collective-permute-done((bf16[48,1280]{1,0:T(8,128)(2,1)}, bf16[48,1280]{1,0:T(8,128)(2,1)S(1)}, u32[]{:S(2)}, u32[]{:S(2)}) %collective-permute-start.27) | collective-permute-done | bytes 122912 | tf_op jit(solution)/shard_map/ppermute | solution.py:428
  132.4 3.2 %pick_rows.3 = (bf16[64,5120]{1,0:T(8,128)(2,1)}, bf16[64,5120]{1,0:T(8,128)(2,1)}) custom-call(s32[1,128]{1,0:T(1,128)} %get-tuple-element.45.base_ref, bf16[48,1280]{1,0:T(8,128)(2,1)} %get-tuple-element.74.refs_0_, bf16[48,1280]{1,0:T(8,128)(2,1)} %copy-done.17, bf16[48,1280]{1,0:T(8,128)(2,1)} %copy-done.18, bf16[48,1280]{1,0:T(8,128)(2,1)} %copy-done.19, ...), custom_call_target="tpu_custom_call" | custom-call | flops 503316480 | bytes 1966080 | tf_op jit(solution)/shard_map/pick_rows/pallas_call | solution.py:386
  136.4 3.7 %collective-permute-start.17 = (bf16[48,512]{1,0:T(8,128)(2,1)S(1)}, bf16[48,512]{1,0:T(8,128)(2,1)S(1)}, u32[]{:S(2)}, u32[]{:S(2)}) collective-permute-start(bf16[48,512]{1,0:T(8,128)(2,1)S(1)} %copy-done.29), channel_id=1, source_target_pairs={{0,2},{1,3},{2,0},{3,1},{4,6},{5,7},{6,4},{7,5},{8,10},{9,11},{10,... | collective-permute-start | bytes 147464 | tf_op jit(solution)/shard_map/ppermute | solution.py:428
  141.1 2.4 %collective-permute-start.19 = (bf16[48,512]{1,0:T(8,128)(2,1)S(1)}, bf16[48,512]{1,0:T(8,128)(2,1)S(1)}, u32[]{:S(2)}, u32[]{:S(2)}) collective-permute-start(bf16[48,512]{1,0:T(8,128)(2,1)S(1)} %copy-done.27), channel_id=1, source_target_pairs={{0,4},{1,5},{2,6},{3,7},{4,0},{5,1},{6,2},{7,3},{8,12},{9,13},{10,... | collective-permute-start | bytes 147464 | tf_op jit(solution)/shard_map/ppermute | solution.py:428
  149.0 2.4 %collective-permute-done.20.refs_5_ = bf16[48,512]{1,0:T(8,128)(2,1)S(1)} collective-permute-done((bf16[48,512]{1,0:T(8,128)(2,1)S(1)}, bf16[48,512]{1,0:T(8,128)(2,1)S(1)}, u32[]{:S(2)}, u32[]{:S(2)}) %collective-permute-start.20) | collective-permute-done | bytes 49184 | tf_op jit(solution)/shard_map/ppermute | solution.py:428
  151.7 2.3 %collective-permute-done.22.refs_7_ = bf16[48,512]{1,0:T(8,128)(2,1)S(1)} collective-permute-done((bf16[48,512]{1,0:T(8,128)(2,1)S(1)}, bf16[48,512]{1,0:T(8,128)(2,1)S(1)}, u32[]{:S(2)}, u32[]{:S(2)}) %collective-permute-start.22) | collective-permute-done | bytes 49184 | tf_op jit(solution)/shard_map/ppermute | solution.py:428
  154.6 2.3 %pick_rows.2 = (bf16[64,2048]{1,0:T(8,128)(2,1)}, bf16[64,2048]{1,0:T(8,128)(2,1)}) custom-call(s32[1,128]{1,0:T(1,128)} %get-tuple-element.45.base_ref, bf16[48,512]{1,0:T(8,128)(2,1)} %get-tuple-element.64.refs_0_, bf16[48,512]{1,0:T(8,128)(2,1)} %copy-done.31, bf16[48,512]{1,0:T(8,128)(2,1)} %copy-done.32, bf16[48,512]{1,0:T(8,128)(2,1)} %copy-done.33, ...), custom_call_target="tpu_custom_call" | custom-call | flops 201326592 | bytes 786432 | tf_op jit(solution)/shard_map/pick_rows/pallas_call | solution.py:386
  159.6 2.9 %mix.1 = bf16[64,7168]{1,0:T(8,128)(2,1)} custom-call(f32[1,64]{1,0:T(1,128)} %bitcast.5, bf16[64,2048]{1,0:T(8,128)(2,1)} %get-tuple-element.72.refs_0_, bf16[64,5120]{1,0:T(8,128)(2,1)} %get-tuple-element.82.refs_1_, bf16[64,2048]{1,0:T(8,128)(2,1)} %copy-done.1, bf16[64,5120]{1,0:T(8,128)(2,1)} %copy-done), custom_call_target="tpu_custom_call" | custom-call | flops 1376256 | bytes 2752512 | tf_op jit(solution)/shard_map/mix/pallas_call | solution.py:412
  (127 shorter events, 26.6 us)
Async XLA Ops:
  8.0 13.2 %collective-permute-start.9 = (bf16[48,1024]{1,0:T(8,128)(2,1)}, bf16[48,1024]{1,0:T(8,128)(2,1)S(1)}, u32[]{:S(2)}, u32[]{:S(2)}) collective-permute-start(bf16[48,1024]{1,0:T(8,128)(2,1)} %get-tuple-element.55), channel_id=1, source_target_pairs={{0,1},{1,0},{2,3},{3,2},{4,5},{5,4},{6,7},{7,6},{8,9},{9,8},{10,11... | collective-permute-start | bytes 294920 | tf_op jit(solution)/shard_map/ppermute | solution.py:428
  10.9 12.5 %collective-permute-start.10 = (bf16[48,1024]{1,0:T(8,128)(2,1)}, bf16[48,1024]{1,0:T(8,128)(2,1)S(1)}, u32[]{:S(2)}, u32[]{:S(2)}) collective-permute-start(bf16[48,1024]{1,0:T(8,128)(2,1)} %get-tuple-element.56), channel_id=1, source_target_pairs={{0,2},{1,3},{2,0},{3,1},{4,6},{5,7},{6,4},{7,5},{8,10},{9,11},{10,... | collective-permute-start | bytes 294920 | tf_op jit(solution)/shard_map/ppermute | solution.py:428
  13.0 12.8 %collective-permute-start.11 = (bf16[48,1024]{1,0:T(8,128)(2,1)}, bf16[48,1024]{1,0:T(8,128)(2,1)S(1)}, u32[]{:S(2)}, u32[]{:S(2)}) collective-permute-start(bf16[48,1024]{1,0:T(8,128)(2,1)} %get-tuple-element.57), channel_id=1, source_target_pairs={{0,3},{1,2},{2,1},{3,0},{4,7},{5,6},{6,5},{7,4},{8,11},{9,10},{10,... | collective-permute-start | bytes 294920 | tf_op jit(solution)/shard_map/ppermute | solution.py:428
  18.1 14.8 %collective-permute-start.12 = (bf16[48,1024]{1,0:T(8,128)(2,1)}, bf16[48,1024]{1,0:T(8,128)(2,1)S(1)}, u32[]{:S(2)}, u32[]{:S(2)}) collective-permute-start(bf16[48,1024]{1,0:T(8,128)(2,1)} %get-tuple-element.58), channel_id=1, source_target_pairs={{0,4},{1,5},{2,6},{3,7},{4,0},{5,1},{6,2},{7,3},{8,12},{9,13},{10,... | collective-permute-start | bytes 294920 | tf_op jit(solution)/shard_map/ppermute | solution.py:428
  20.7 13.0 %collective-permute-start.13 = (bf16[48,1024]{1,0:T(8,128)(2,1)}, bf16[48,1024]{1,0:T(8,128)(2,1)S(1)}, u32[]{:S(2)}, u32[]{:S(2)}) collective-permute-start(bf16[48,1024]{1,0:T(8,128)(2,1)} %get-tuple-element.59), channel_id=1, source_target_pairs={{0,5},{1,4},{2,7},{3,6},{4,1},{5,0},{6,3},{7,2},{8,13},{9,12},{10,... | collective-permute-start | bytes 294920 | tf_op jit(solution)/shard_map/ppermute | solution.py:428
  21.2 13.4 %collective-permute-start.14 = (bf16[48,1024]{1,0:T(8,128)(2,1)}, bf16[48,1024]{1,0:T(8,128)(2,1)S(1)}, u32[]{:S(2)}, u32[]{:S(2)}) collective-permute-start(bf16[48,1024]{1,0:T(8,128)(2,1)} %get-tuple-element.60), channel_id=1, source_target_pairs={{0,6},{1,7},{2,4},{3,5},{4,2},{5,3},{6,0},{7,1},{8,14},{9,15},{10,... | collective-permute-start | bytes 294920 | tf_op jit(solution)/shard_map/ppermute | solution.py:428
  23.4 14.7 %collective-permute-start.15 = (bf16[48,1024]{1,0:T(8,128)(2,1)}, bf16[48,1024]{1,0:T(8,128)(2,1)S(1)}, u32[]{:S(2)}, u32[]{:S(2)}) collective-permute-start(bf16[48,1024]{1,0:T(8,128)(2,1)} %get-tuple-element.61), channel_id=1, source_target_pairs={{0,7},{1,6},{2,5},{3,4},{4,3},{5,2},{6,1},{7,0},{8,15},{9,14},{10,... | collective-permute-start | bytes 294920 | tf_op jit(solution)/shard_map/ppermute | solution.py:428
  25.8 34.7 %collective-permute-start.4 = (bf16[48,768]{1,0:T(8,128)(2,1)}, bf16[48,768]{1,0:T(8,128)(2,1)S(1)}, u32[]{:S(2)}, u32[]{:S(2)}) collective-permute-start(bf16[48,768]{1,0:T(8,128)(2,1)} %get-tuple-element.49), channel_id=1, source_target_pairs={{0,3},{1,2},{2,1},{3,0},{4,7},{5,6},{6,5},{7,4},{8,11},{9,10},{10,... | collective-permute-start | bytes 221192 | tf_op jit(solution)/shard_map/ppermute | solution.py:428
  32.9 27.6 %collective-permute-start.5 = (bf16[48,768]{1,0:T(8,128)(2,1)}, bf16[48,768]{1,0:T(8,128)(2,1)S(1)}, u32[]{:S(2)}, u32[]{:S(2)}) collective-permute-start(bf16[48,768]{1,0:T(8,128)(2,1)} %get-tuple-element.50), channel_id=1, source_target_pairs={{0,4},{1,5},{2,6},{3,7},{4,0},{5,1},{6,2},{7,3},{8,12},{9,13},{10,... | collective-permute-start | bytes 221192 | tf_op jit(solution)/shard_map/ppermute | solution.py:428
  33.7 26.9 %collective-permute-start.6 = (bf16[48,768]{1,0:T(8,128)(2,1)}, bf16[48,768]{1,0:T(8,128)(2,1)S(1)}, u32[]{:S(2)}, u32[]{:S(2)}) collective-permute-start(bf16[48,768]{1,0:T(8,128)(2,1)} %get-tuple-element.51), channel_id=1, source_target_pairs={{0,5},{1,4},{2,7},{3,6},{4,1},{5,0},{6,3},{7,2},{8,13},{9,12},{10,... | collective-permute-start | bytes 221192 | tf_op jit(solution)/shard_map/ppermute | solution.py:428
  34.6 26.0 %collective-permute-start.7 = (bf16[48,768]{1,0:T(8,128)(2,1)}, bf16[48,768]{1,0:T(8,128)(2,1)S(1)}, u32[]{:S(2)}, u32[]{:S(2)}) collective-permute-start(bf16[48,768]{1,0:T(8,128)(2,1)} %get-tuple-element.52), channel_id=1, source_target_pairs={{0,6},{1,7},{2,4},{3,5},{4,2},{5,3},{6,0},{7,1},{8,14},{9,15},{10,... | collective-permute-start | bytes 221192 | tf_op jit(solution)/shard_map/ppermute | solution.py:428
  38.1 22.5 %collective-permute-start.8 = (bf16[48,768]{1,0:T(8,128)(2,1)}, bf16[48,768]{1,0:T(8,128)(2,1)S(1)}, u32[]{:S(2)}, u32[]{:S(2)}) collective-permute-start(bf16[48,768]{1,0:T(8,128)(2,1)} %get-tuple-element.53), channel_id=1, source_target_pairs={{0,7},{1,6},{2,5},{3,4},{4,3},{5,2},{6,1},{7,0},{8,15},{9,14},{10,... | collective-permute-start | bytes 221192 | tf_op jit(solution)/shard_map/ppermute | solution.py:428
  103.7 11.4 %collective-permute-start.23 = (bf16[48,1280]{1,0:T(8,128)(2,1)}, bf16[48,1280]{1,0:T(8,128)(2,1)S(1)}, u32[]{:S(2)}, u32[]{:S(2)}) collective-permute-start(bf16[48,1280]{1,0:T(8,128)(2,1)} %get-tuple-element.75), channel_id=1, source_target_pairs={{0,1},{1,0},{2,3},{3,2},{4,5},{5,4},{6,7},{7,6},{8,9},{9,8},{10,11... | collective-permute-start | bytes 368648 | tf_op jit(solution)/shard_map/ppermute | solution.py:428
  103.7 13.4 %collective-permute-start.24 = (bf16[48,1280]{1,0:T(8,128)(2,1)}, bf16[48,1280]{1,0:T(8,128)(2,1)S(1)}, u32[]{:S(2)}, u32[]{:S(2)}) collective-permute-start(bf16[48,1280]{1,0:T(8,128)(2,1)} %get-tuple-element.76), channel_id=1, source_target_pairs={{0,2},{1,3},{2,0},{3,1},{4,6},{5,7},{6,4},{7,5},{8,10},{9,11},{10,... | collective-permute-start | bytes 368648 | tf_op jit(solution)/shard_map/ppermute | solution.py:428
  111.2 8.5 %collective-permute-start.25 = (bf16[48,1280]{1,0:T(8,128)(2,1)}, bf16[48,1280]{1,0:T(8,128)(2,1)S(1)}, u32[]{:S(2)}, u32[]{:S(2)}) collective-permute-start(bf16[48,1280]{1,0:T(8,128)(2,1)} %get-tuple-element.77), channel_id=1, source_target_pairs={{0,3},{1,2},{2,1},{3,0},{4,7},{5,6},{6,5},{7,4},{8,11},{9,10},{10,... | collective-permute-start | bytes 368648 | tf_op jit(solution)/shard_map/ppermute | solution.py:428
  111.3 17.0 %collective-permute-start.26 = (bf16[48,1280]{1,0:T(8,128)(2,1)}, bf16[48,1280]{1,0:T(8,128)(2,1)S(1)}, u32[]{:S(2)}, u32[]{:S(2)}) collective-permute-start(bf16[48,1280]{1,0:T(8,128)(2,1)} %get-tuple-element.78), channel_id=1, source_target_pairs={{0,4},{1,5},{2,6},{3,7},{4,0},{5,1},{6,2},{7,3},{8,12},{9,13},{10,... | collective-permute-start | bytes 368648 | tf_op jit(solution)/shard_map/ppermute | solution.py:428
  114.3 17.4 %collective-permute-start.27 = (bf16[48,1280]{1,0:T(8,128)(2,1)}, bf16[48,1280]{1,0:T(8,128)(2,1)S(1)}, u32[]{:S(2)}, u32[]{:S(2)}) collective-permute-start(bf16[48,1280]{1,0:T(8,128)(2,1)} %get-tuple-element.79), channel_id=1, source_target_pairs={{0,5},{1,4},{2,7},{3,6},{4,1},{5,0},{6,3},{7,2},{8,13},{9,12},{10,... | collective-permute-start | bytes 368648 | tf_op jit(solution)/shard_map/ppermute | solution.py:428
  115.1 16.6 %collective-permute-start.28 = (bf16[48,1280]{1,0:T(8,128)(2,1)}, bf16[48,1280]{1,0:T(8,128)(2,1)S(1)}, u32[]{:S(2)}, u32[]{:S(2)}) collective-permute-start(bf16[48,1280]{1,0:T(8,128)(2,1)} %get-tuple-element.80), channel_id=1, source_target_pairs={{0,6},{1,7},{2,4},{3,5},{4,2},{5,3},{6,0},{7,1},{8,14},{9,15},{10,... | collective-permute-start | bytes 368648 | tf_op jit(solution)/shard_map/ppermute | solution.py:428
  117.1 14.6 %collective-permute-start.29 = (bf16[48,1280]{1,0:T(8,128)(2,1)}, bf16[48,1280]{1,0:T(8,128)(2,1)S(1)}, u32[]{:S(2)}, u32[]{:S(2)}) collective-permute-start(bf16[48,1280]{1,0:T(8,128)(2,1)} %get-tuple-element.81), channel_id=1, source_target_pairs={{0,7},{1,6},{2,5},{3,4},{4,3},{5,2},{6,1},{7,0},{8,15},{9,14},{10,... | collective-permute-start | bytes 368648 | tf_op jit(solution)/shard_map/ppermute | solution.py:428
  135.7 23.0 %collective-permute-start.31 = (bf16[64,5120]{1,0:T(8,128)(2,1)}, bf16[64,5120]{1,0:T(8,128)(2,1)S(1)}, u32[]{:S(2)}, u32[]{:S(2)}) collective-permute-start(bf16[64,5120]{1,0:T(8,128)(2,1)} %get-tuple-element.84), channel_id=1, source_target_pairs={{0,8},{8,0},{1,9},{9,1},{2,10},{10,2},{3,11},{11,3},{4,12},{12,4},... | collective-permute-start | bytes 1966088 | tf_op jit(solution)/shard_map/ppermute | solution.py:435
  135.7 7.9 %collective-permute-start.16 = (bf16[48,512]{1,0:T(8,128)(2,1)S(1)}, bf16[48,512]{1,0:T(8,128)(2,1)S(1)}, u32[]{:S(2)}, u32[]{:S(2)}) collective-permute-start(bf16[48,512]{1,0:T(8,128)(2,1)S(1)} %copy-done.30), channel_id=1, source_target_pairs={{0,1},{1,0},{2,3},{3,2},{4,5},{5,4},{6,7},{7,6},{8,9},{9,8},{10,11... | collective-permute-start | bytes 147464 | tf_op jit(solution)/shard_map/ppermute | solution.py:428
  136.4 8.8 %collective-permute-start.17 = (bf16[48,512]{1,0:T(8,128)(2,1)S(1)}, bf16[48,512]{1,0:T(8,128)(2,1)S(1)}, u32[]{:S(2)}, u32[]{:S(2)}) collective-permute-start(bf16[48,512]{1,0:T(8,128)(2,1)S(1)} %copy-done.29), channel_id=1, source_target_pairs={{0,2},{1,3},{2,0},{3,1},{4,6},{5,7},{6,4},{7,5},{8,10},{9,11},{10,... | collective-permute-start | bytes 147464 | tf_op jit(solution)/shard_map/ppermute | solution.py:428
  141.1 7.9 %collective-permute-start.19 = (bf16[48,512]{1,0:T(8,128)(2,1)S(1)}, bf16[48,512]{1,0:T(8,128)(2,1)S(1)}, u32[]{:S(2)}, u32[]{:S(2)}) collective-permute-start(bf16[48,512]{1,0:T(8,128)(2,1)S(1)} %copy-done.27), channel_id=1, source_target_pairs={{0,4},{1,5},{2,6},{3,7},{4,0},{5,1},{6,2},{7,3},{8,12},{9,13},{10,... | collective-permute-start | bytes 147464 | tf_op jit(solution)/shard_map/ppermute | solution.py:428
  143.6 7.8 %collective-permute-start.20 = (bf16[48,512]{1,0:T(8,128)(2,1)S(1)}, bf16[48,512]{1,0:T(8,128)(2,1)S(1)}, u32[]{:S(2)}, u32[]{:S(2)}) collective-permute-start(bf16[48,512]{1,0:T(8,128)(2,1)S(1)} %copy-done.26), channel_id=1, source_target_pairs={{0,5},{1,4},{2,7},{3,6},{4,1},{5,0},{6,3},{7,2},{8,13},{9,12},{10,... | collective-permute-start | bytes 147464 | tf_op jit(solution)/shard_map/ppermute | solution.py:428
  (46 other events, 682.6 us)

commit v2 on v0

--- a/solution.py
+++ b/solution.py
@@ -1,10 +1,21 @@
+import functools
+
 import jax
 import jax.numpy as jnp
+import numpy as np
 from jax import lax
+from jax.experimental import pallas as pl
+from jax.experimental.pallas import tpu as pltpu
 from jax.sharding import PartitionSpec as P
 
 FF = 2048
 CAP = 6
+FOLD = 4
+STEP = 512
+DEPTH = 8
+DISPATCH = (1280, 512)
+RETURN = (256, 1536)
+VMEM_BYTES = 56 * 1024 * 1024
 
 
 def route_tables(experts, replicas, gates, placement, slot_count, capacity):
@@ -30,8 +41,10 @@
     return (scatter, combine)
 
 
-def per_device(tokens, experts, replicas, gates, placement, gate_weight, up_weight, down_weight):
-    tok_rows, model_width = tokens.shape
+def per_device_general(
+    tokens, experts, replicas, gates, placement, gate_weight, up_weight, down_weight
+):
+    model_width = tokens.shape[1]
     hidden_dev = gate_weight.shape[2]
     group_size = FF // hidden_dev
     devices_all = lax.axis_size(("node", "local"))
@@ -68,6 +81,337 @@
     return mixed.astype(jnp.bfloat16)
 
 
+def params(**kw):
+    return pltpu.CompilerParams(vmem_limit_bytes=VMEM_BYTES, **kw)
+
+
+VMEM = pl.BlockSpec(memory_space=pltpu.VMEM)
+SMEM = pl.BlockSpec(memory_space=pltpu.SMEM)
+HBM = pl.BlockSpec(memory_space=pl.ANY)
+
+
+def cost(flops, size):
+    return pl.CostEstimate(flops=int(flops), bytes_accessed=int(size), transcendentals=0)
+
+
+def fold_matrix(groups):
+    g, q, c = np.meshgrid(np.arange(groups), np.arange(FOLD), np.arange(CAP), indexing="ij")
+    size = groups * FOLD * CAP
+    matrix = np.zeros((size, size), np.float32)
+    matrix[
+        (q * groups * CAP + g * CAP + c).ravel(), (g * FOLD * CAP + q * CAP + c).ravel()
+    ] = 1.0
+    return matrix
+
+
+def dispatch_kernel(widths, place_ref, experts_ref, replicas_ref, tokens_ref, base_ref, *pieces):
+    tok = tokens_ref.shape[0]
+    rows = pieces[0].shape[0]
+    slots = rows // (FOLD * CAP)
+    experts, replicas = experts_ref[...], replicas_ref[...]
+    slot = jnp.zeros((1, tok), jnp.int32)
+    for r in range(place_ref.shape[0]):
+        for e in range(place_ref.shape[1]):
+            slot = jnp.where((experts == e) & (replicas == r), place_ref[r, e], slot)
+    hit = lax.broadcasted_iota(jnp.int32, (slots, tok), 0) == slot
+    earlier = lax.broadcasted_iota(jnp.int32, (tok, tok), 0) < lax.broadcasted_iota(
+        jnp.int32, (tok, tok), 1
+    )
+    before = jnp.dot(
+        hit.astype(jnp.bfloat16), earlier.astype(jnp.bfloat16), preferred_element_type=jnp.float32
+    )
+    rank = jnp.sum(jnp.where(hit, before, 0.0), axis=0, keepdims=True).astype(jnp.int32)
+    base = slot * (FOLD * CAP) + rank
+    base_ref[...] = base
+    row = lax.broadcasted_iota(jnp.int32, (rows, tok), 0)
+    select = jnp.concatenate(
+        [(row == base + q * CAP).astype(jnp.bfloat16) for q in range(FOLD)], axis=1
+    )
+    start = 0
+    for piece, width in zip(pieces, widths):
+        folded = jnp.concatenate(
+            [tokens_ref[:, start + q * width : start + (q + 1) * width] for q in range(FOLD)],
+            axis=0,
+        )
+        piece[...] = jnp.dot(select, folded, preferred_element_type=jnp.float32).astype(
+            jnp.bfloat16
+        )
+        start += FOLD * width
+
+
+def dispatch(placement, experts, replicas, tokens, slots):
+    tok, model = tokens.shape
+    rows = slots * FOLD * CAP
+    out_shape = [jax.ShapeDtypeStruct((1, tok), jnp.int32)] + [
+        jax.ShapeDtypeStruct((rows, width), jnp.bfloat16) for width in DISPATCH
+    ]
+    return pl.pallas_call(
+        functools.partial(dispatch_kernel, DISPATCH),
+        out_shape=out_shape,
+        in_specs=[SMEM, VMEM, VMEM, VMEM],
+        out_specs=[VMEM] * len(out_shape),
+        compiler_params=params(),
+        cost_estimate=cost(2 * rows * tok * model, 5 * tok * model),
+        name="dispatch",
+    )(placement.T, experts.reshape(1, tok), replicas.reshape(1, tok), tokens)
+
+
+class Stream:
+    def __init__(self, buffer, sems, tiles):
+        self.depth = buffer.shape[0]
+        self.buffer = buffer
+        self.copies = []
+        for n, tile in enumerate(tiles):
+            slot = n % self.depth
+            self.copies.append(
+                pltpu.make_async_copy(tile, buffer.at[slot], sems.at[slot])
+            )
+        self.begun = 0
+
+    def ahead(self, upto):
+        while self.begun < min(upto, len(self.copies)):
+            self.copies[self.begun].start()
+            self.begun += 1
+
+    def take(self, n):
+        self.ahead(n + 1)
+        self.copies[n].wait()
+        return self.buffer[n % self.depth]
+
+    def free(self, n):
+        self.ahead(n + 1 + self.depth)
+
+
+def unfold(block_ref, order_ref, x_ref):
+    rows, width = x_ref.shape[0], block_ref.shape[1]
+    value = jnp.dot(order_ref[...], block_ref[...], preferred_element_type=jnp.float32)
+    value = value.astype(jnp.bfloat16)
+    for q in range(FOLD):
+        x_ref[:, q * width : (q + 1) * width] = value[q * rows : (q + 1) * rows]
+
+
+def refold(o_ref, order_ref, block_ref):
+    width = block_ref.shape[1]
+    value = jnp.concatenate(
+        [o_ref[:, q * width : (q + 1) * width] for q in range(FOLD)], axis=0
+    )
+    block_ref[...] = jnp.dot(
+        order_ref[...], value, preferred_element_type=jnp.float32
+    ).astype(jnp.bfloat16)
+
+
+def project(x_ref, tiles, accg_ref, accu_ref, fresh):
+    for n in range(x_ref.shape[1] // STEP):
+        x = x_ref[:, n * STEP : (n + 1) * STEP]
+        for m, acc in enumerate((accg_ref, accu_ref)):
+            value = jnp.dot(x, tiles.take(2 * n + m), preferred_element_type=jnp.float32)
+            acc[...] = value if fresh and n == 0 else acc[...] + value
+            tiles.free(2 * n + m)
+
+
+def in_tiles(wg_ref, wu_ref, start, count):
+    return [
+        w.at[0, pl.ds(start + n * STEP, STEP)] for n in range(count) for w in (wg_ref, wu_ref)
+    ]
+
+
+def out_tiles(wd_ref, start, count):
+    return [wd_ref.at[0, :, pl.ds(start + n * STEP, STEP)] for n in range(count)]
+
+
+def first_kernel(start, order_ref, block_ref, wg_ref, wu_ref, accg_ref, accu_ref, x_ref, w_ref, sem):
+    tiles = Stream(w_ref, sem, in_tiles(wg_ref, wu_ref, start, x_ref.shape[1] // STEP))
+    tiles.ahead(tiles.depth)
+    unfold(block_ref, order_ref, x_ref)
+    project(x_ref, tiles, accg_ref, accu_ref, True)
+
+
+def first_part(order, block, gate_weight, up_weight, start):
+    rows = block.shape[0] // FOLD
+    model, hidden = FOLD * block.shape[1], gate_weight.shape[2]
+    acc = jax.ShapeDtypeStruct((rows, hidden), jnp.float32)
+    return pl.pallas_call(
+        functools.partial(first_kernel, start),
+        out_shape=[acc, acc],
+        in_specs=[VMEM, VMEM, HBM, HBM],
+        out_specs=[VMEM, VMEM],
+        scratch_shapes=[
+            pltpu.VMEM((rows, model), jnp.bfloat16),
+            pltpu.VMEM((DEPTH, STEP, hidden), jnp.bfloat16),
+            pltpu.SemaphoreType.DMA((DEPTH,)),
+        ],
+        compiler_params=params(),
+        cost_estimate=cost(4 * rows * model * hidden, 4 * model * hidden),
+        name="first_part",
+    )(order, block, gate_weight, up_weight)
+
+
+def down(hidden_ref, tiles, o_ref):
+    for n in range(o_ref.shape[1] // STEP):
+        o_ref[:, n * STEP : (n + 1) * STEP] = jnp.dot(
+            hidden_ref[...], tiles.take(n), preferred_element_type=jnp.float32
+        ).astype(jnp.bfloat16)
+        tiles.free(n)
+
+
+def middle_kernel(
+    start,
+    order_ref,
+    back_ref,
+    block_ref,
+    ing_ref,
+    inu_ref,
+    wg_ref,
+    wu_ref,
+    wd_ref,
+    hidden_ref,
+    out_ref,
+    x_ref,
+    accg_ref,
+    accu_ref,
+    o_ref,
+    w_ref,
+    d_ref,
+    sem,
+    dsem,
+):
+    tiles = Stream(w_ref, sem, in_tiles(wg_ref, wu_ref, start, x_ref.shape[1] // STEP))
+    outs = Stream(d_ref, dsem, out_tiles(wd_ref, 0, o_ref.shape[1] // STEP))
+    tiles.ahead(tiles.depth)
+    outs.ahead(outs.depth)
+    unfold(block_ref, order_ref, x_ref)
+    accg_ref[...] = ing_ref[...]
+    accu_ref[...] = inu_ref[...]
+    project(x_ref, tiles, accg_ref, accu_ref, False)
+    gate_val = accg_ref[...]
+    hidden_ref[...] = (gate_val / (1.0 + jnp.exp(-gate_val)) * accu_ref[...]).astype(jnp.bfloat16)
+    down(hidden_ref, outs, o_ref)
+    refold(o_ref, back_ref, out_ref)
+
+
+def middle_part(order, back, block, accs, gate_weight, up_weight, down_weight, start):
+    rows = block.shape[0] // FOLD
+    model, hidden = FOLD * block.shape[1], gate_weight.shape[2]
+    model_out = FOLD * RETURN[0]
+    out_depth = min(DEPTH // 2, model_out // STEP)
+    return pl.pallas_call(
+        functools.partial(middle_kernel, start),
+        out_shape=[
+            jax.ShapeDtypeStruct((rows, hidden), jnp.bfloat16),
+            jax.ShapeDtypeStruct((block.shape[0], RETURN[0]), jnp.bfloat16),
+        ],
+        in_specs=[VMEM] * 5 + [HBM] * 3,
+        out_specs=[VMEM, VMEM],
+        scratch_shapes=[
+            pltpu.VMEM((rows, model), jnp.bfloat16),
+            pltpu.VMEM((rows, hidden), jnp.float32),
+            pltpu.VMEM((rows, hidden), jnp.float32),
+            pltpu.VMEM((rows, model_out), jnp.bfloat16),
+            pltpu.VMEM((DEPTH, STEP, hidden), jnp.bfloat16),
+            pltpu.VMEM((out_depth, hidden, STEP), jnp.bfloat16),
+            pltpu.SemaphoreType.DMA((DEPTH,)),
+            pltpu.SemaphoreType.DMA((out_depth,)),
+        ],
+        compiler_params=params(),
+        cost_estimate=cost(
+            2 * rows * (2 * model + model_out) * hidden, 2 * (2 * model + model_out) * hidden
+        ),
+        name="middle_part",
+    )(order, back, block, *accs, gate_weight, up_weight, down_weight)
+
+
+def last_kernel(start, back_ref, hidden_ref, wd_ref, out_ref, o_ref, d_ref, dsem):
+    outs = Stream(d_ref, dsem, out_tiles(wd_ref, start, o_ref.shape[1] // STEP))
+    outs.ahead(outs.depth)
+    down(hidden_ref, outs, o_ref)
+    refold(o_ref, back_ref, out_ref)
+
+
+def last_part(back, hidden, down_weight, start, width):
+    rows, inner = hidden.shape
+    model_out = FOLD * width
+    return pl.pallas_call(
+        functools.partial(last_kernel, start),
+        out_shape=jax.ShapeDtypeStruct((FOLD * rows, width), jnp.bfloat16),
+        in_specs=[VMEM, VMEM, HBM],
+        out_specs=VMEM,
+        scratch_shapes=[
+            pltpu.VMEM((rows, model_out), jnp.bfloat16),
+            pltpu.VMEM((DEPTH, inner, STEP), jnp.bfloat16),
+            pltpu.SemaphoreType.DMA((DEPTH,)),
+        ],
+        compiler_params=params(),
+        cost_estimate=cost(2 * rows * model_out * inner, 2 * model_out * inner),
+        name="last_part",
+    )(back, hidden, down_weight)
+
+
+def column(row):
+    n = row.shape[1]
+    eye = lax.broadcasted_iota(jnp.int32, (n, n), 0) == lax.broadcasted_iota(jnp.int32, (n, n), 1)
+    return jnp.sum(jnp.where(eye, row, jnp.zeros_like(row)), axis=1, keepdims=True)
+
+
+def finish_kernel(base_ref, gates_ref, *refs):
+    pieces, out_ref = refs[:-1], refs[-1]
+    base = column(base_ref[...])
+    gate = column(gates_ref[...])
+    lane = lax.broadcasted_iota(jnp.int32, (base.shape[0], pieces[0].shape[0]), 1)
+    select = [(lane == base + q * CAP).astype(jnp.bfloat16) for q in range(FOLD)]
+    start = 0
+    for piece in pieces:
+        width = piece.shape[1]
+        for q in range(FOLD):
+            value = jnp.dot(select[q], piece[...], preferred_element_type=jnp.float32)
+            out_ref[:, start : start + width] = (gate * value).astype(jnp.bfloat16)
+            start += width
+
+
+def finish(base, gates, pieces):
+    tok = base.shape[1]
+    model = FOLD * sum(p.shape[1] for p in pieces)
+    return pl.pallas_call(
+        finish_kernel,
+        out_shape=jax.ShapeDtypeStruct((tok, model), jnp.bfloat16),
+        in_specs=[VMEM] * (2 + len(pieces)),
+        out_specs=VMEM,
+        compiler_params=params(),
+        cost_estimate=cost(2 * tok * model * 384, 5 * tok * model),
+        name="finish",
+    )(base, gates.reshape(1, tok), *pieces)
+
+
+def swap(block, slots):
+    rows, width = block.shape
+    out = lax.all_to_all(
+        block.reshape(slots, rows // slots, width),
+        ("node", "local"),
+        split_axis=0,
+        concat_axis=0,
+        tiled=True,
+    )
+    return out.reshape(rows, width)
+
+
+def per_device_folded(
+    tokens, experts, replicas, gates, placement, gate_weight, up_weight, down_weight
+):
+    slots = lax.axis_size(("node", "local"))
+    matrix = fold_matrix(slots)
+    order = jnp.asarray(matrix, jnp.bfloat16)
+    back = jnp.asarray(matrix.T, jnp.bfloat16)
+    base, *pieces = dispatch(placement, experts, replicas, tokens, slots)
+    arrived = [swap(piece, slots) for piece in pieces]
+    accs = first_part(order, arrived[0], gate_weight, up_weight, 0)
+    hidden, back_first = middle_part(
+        order, back, arrived[1], accs, gate_weight, up_weight, down_weight, FOLD * DISPATCH[0]
+    )
+    returned = [swap(back_first, slots)]
+    back_second = last_part(back, hidden, down_weight, FOLD * RETURN[0], RETURN[1])
+    returned.append(swap(back_second, slots))
+    return finish(base, gates, returned)
+
+
 def solution(mesh):
     in_specs = (
         P(("parts", "node", "local"), None),
@@ -80,6 +424,16 @@
         P(("node", "local"), None, None),
     )
     out_specs = P(("parts", "node", "local"), None)
+
+    def per_device(*args):
+        folded = (
+            mesh.shape["node"] * mesh.shape["local"] == 16
+            and args[1].shape[1] == 1
+            and args[5].shape[2] == FF
+            and args[0].shape[1] == FOLD * sum(DISPATCH)
+        )
+        return (per_device_folded if folded else per_device_general)(*args)
+
     return jax.shard_map(
         per_device, mesh=mesh, in_specs=in_specs, out_specs=out_specs, check_vma=False
     )

time: 146 us -> 125 us (0.86)
  Pallas kernels: 0 us -> 45.1 us
  waiting for transfers between devices: 42 us -> 0.01 us
  matrix products: 38.5 us -> 0 us
  blocking collectives: 51.3 us -> 69.4 us
  local copies, waits for them, and re-layouts: 8.16 us -> 0.76 us
  starting transfers between devices: 3.84 us -> 9.49 us
  other arithmetic: 1.97 us -> 0 us
    pallas_call x0 -> x5, Pallas kernels: none -> 45.1 us  [the longest x1 16 us: first_part(): pl.pallas_call(functools.partial(first_kernel, start), out_shape=[acc, ac...]
    all_to_all x1 -> x2, waiting for transfers between devices: 42 us -> 0.01 us  [swap(): lax.all_to_all(block.reshape(slots, rows // slots, width), ('node', 'loca...]
    dot_general x4 -> x0, matrix products: 38.5 us -> none  [the longest x1 21.8 us: per_device(): jnp.dot(hidden, down_weight[0], preferred_element_type=jnp.float32)]
    all_to_all x1 -> x2, blocking collectives: 51.3 us -> 69.4 us  [swap(): lax.all_to_all(block.reshape(slots, rows // slots, width), ('node', 'loca...]
    reshape x3 -> x0, local copies, waits for them, and re-layouts: 5.68 us -> none  [the longest x1 2.6 us: per_device(): partial_value = jnp.dot(hidden, down_weight[0], preferred_element_type=jn...]
    all_to_all x1 -> x2, starting transfers between devices: 3.84 us -> 9.49 us  [swap(): lax.all_to_all(block.reshape(slots, rows // slots, width), ('node', 'loca...]
    another operation x1 -> x0, local copies, waits for them, and re-layouts: 1.62 us -> none  [per_device(): sending = jnp.repeat(outgoing, group_size, axis=0)]
  transfers between devices with their start and end apart: 1 -> 2, of which waited for: 1 -> 0; matrix products, arithmetic and copies ran while one was open for 0% -> 0% of each run, Pallas kernels for 0% -> 22%
where the time goes in v2:
time: 125 us
  blocking collectives  69.4 us (56%)
  Pallas kernels  45.1 us (36%)
  starting transfers between devices  9.49 us (8%)
    all_to_all x2, blocking collectives, swap(): lax.all_to_all(block.reshape(slots, rows // slots, width), ('node', 'loca...  69.4 us
    pallas_call x1, Pallas kernels, first_part(): pl.pallas_call(functools.partial(first_kernel, start), out_shape=[acc, ac...  16 us
    pallas_call x1, Pallas kernels, last_part(): pl.pallas_call(functools.partial(last_kernel, start), out_shape=jax.Shape...  11.9 us
    pallas_call x1, Pallas kernels, middle_part(): pl.pallas_call(functools.partial(middle_kernel, start), out_shape=[jax.Sh...  10.7 us
    all_to_all x2, starting transfers between devices, swap(): lax.all_to_all(block.reshape(slots, rows // slots, width), ('node', 'loca...  9.49 us
    pallas_call x1, Pallas kernels, finish(): pl.pallas_call(finish_kernel, out_shape=jax.ShapeDtypeStruct((tok, model)...  3.49 us
    pallas_call x1, Pallas kernels, dispatch(): pl.pallas_call(functools.partial(dispatch_kernel, DISPATCH), out_shape=ou...  2.95 us
  transfers between devices with their start and end apart: 2, of which 0 were waited for; matrix products, arithmetic and copies ran while one was open for 0% of the time, Pallas kernels for 22%

profile of v2, /device:TPU:0, one launch (start us, length us, event | category | flops | bytes accessed | tf_op | source)
XLA Modules:
  0.0 124.8 jit_solution(15607728811673617790)
XLA Ops:
  0.0 2.9 %dispatch.1 = (s32[1,64]{1,0:T(1,128)}, bf16[384,1280]{1,0:T(8,128)(2,1)}, bf16[384,512]{1,0:T(8,128)(2,1)}) custom-call(s32[2,12]{1,0:T(2,128)} %bitcast.21, s32[1,64]{1,0:T(1,128)} %bitcast.22, s32[1,64]{1,0:T(1,128)} %bitcast.23, bf16[64,7168]{1,0:T(8,128)(2,1)} %tokens_ref.1), custom_call_target="tpu_custom_call" | custom-call | flops 352321536 | bytes 2293760 | tf_op jit(solution)/shard_map/dispatch/pallas_call | solution.py:148
  3.0 33.1 %all_to_all.20 = bf16[16,24,1280]{2,1,0:T(8,128)(2,1)} all-to-all(bf16[16,24,1280]{2,1,0:T(8,128)(2,1)} %bitcast.16), channel_id=1, replica_groups=mesh['parts'=2,'node'=2,'local'=8] {'node','local'}, dimensions={0} | all-to-all | bytes 1966080 | tf_op jit(solution)/shard_map/all_to_all | solution.py:386
  36.1 3.6 %all-to-all-start = ((bf16[16,24,512]{2,1,0:T(8,128)(2,1)}), bf16[16,24,512]{2,1,0:T(8,128)(2,1)S(1)}, u32[]{:S(2)}, u32[]{:S(2)}) async-start(bf16[16,24,512]{2,1,0:T(8,128)(2,1)} %bitcast.18), calls=%async_computation | async-start | bytes 786432 | tf_op jit(solution)/shard_map/all_to_all | solution.py:386
  39.7 16.0 %first_part.1 = (f32[96,2048]{1,0:T(8,128)}, f32[96,2048]{1,0:T(8,128)}) custom-call(bf16[384,384]{1,0:T(8,128)(2,1)} %constant.4.clone.order_ref, bf16[384,1280]{1,0:T(8,128)(2,1)} %bitcast.14, bf16[1,7168,2048]{2,1,0:T(8,128)(2,1)} %wg_ref.3, bf16[1,7168,2048]{2,1,0:T(8,128)(2,1)} %wu_ref.3), custom_call_target="tpu_custom_call" | custom-call | flops 4026531840 | bytes 41943040 | tf_op jit(solution)/shard_map/first_part/pallas_call | solution.py:233
  55.7 0.0 all-to-all-done
  55.7 0.0 copy-start
  55.7 0.8 copy-done
  56.4 10.7 %middle_part.1 = (bf16[96,2048]{1,0:T(8,128)(2,1)}, bf16[384,256]{1,0:T(8,128)(2,1)}) custom-call(bf16[384,384]{1,0:T(8,128)(2,1)} %constant.4.clone.order_ref, bf16[384,384]{1,0:T(8,128)(2,1)} %constant.5.clone.back_ref, bf16[384,512]{1,0:T(8,128)(2,1)} %bitcast.15, f32[96,2048]{1,0:T(8,128)} %get-tuple-element.15.ing_ref, ...), custom_call_target="tpu_custom_call" | custom-call | flops 2013265920 | bytes 20971520 | tf_op jit(solution)/shard_map/middle_part/pallas_call | solution.py:297
  67.2 5.9 %all-to-all-start.2 = ((bf16[16,24,256]{2,1,0:T(8,128)(2,1)}), bf16[16,24,256]{2,1,0:T(8,128)(2,1)S(1)}, u32[]{:S(2)}, u32[]{:S(2)}) async-start(bf16[16,24,256]{2,1,0:T(8,128)(2,1)} %bitcast.19), calls=%async_computation.2 | async-start | bytes 393216 | tf_op jit(solution)/shard_map/all_to_all | solution.py:386
  73.1 11.9 %last_part.1 = bf16[384,1536]{1,0:T(8,128)(2,1)} custom-call(bf16[384,384]{1,0:T(8,128)(2,1)} %constant.5.clone.back_ref, bf16[96,2048]{1,0:T(8,128)(2,1)} %get-tuple-element.18.hidden_ref, bf16[1,2048,7168]{2,1,0:T(8,128)(2,1)} %wd_ref.3), custom_call_target="tpu_custom_call" | custom-call | flops 2415919104 | bytes 25165824 | tf_op jit(solution)/shard_map/last_part/pallas_call | solution.py:333
  85.1 0.0 all-to-all-done.2
  85.1 0.0 copy-start.1
  85.1 36.2 %all_to_all.21 = bf16[16,24,1536]{2,1,0:T(8,128)(2,1)} all-to-all(bf16[16,24,1536]{2,1,0:T(8,128)(2,1)} %bitcast.12), channel_id=1, replica_groups=mesh['parts'=2,'node'=2,'local'=8] {'node','local'}, dimensions={0} | all-to-all | bytes 2359296 | tf_op jit(solution)/shard_map/all_to_all | solution.py:386
  121.3 0.0 copy-done.1
  121.3 3.5 %finish.1 = bf16[64,7168]{1,0:T(8,128)(2,1)} custom-call(s32[1,64]{1,0:T(1,128)} %get-tuple-element.12.base_ref, f32[1,64]{1,0:T(1,128)} %bitcast.20, bf16[384,256]{1,0:T(8,128)(2,1)} %bitcast.17, bf16[384,1536]{1,0:T(8,128)(2,1)} %bitcast.13), custom_call_target="tpu_custom_call" | custom-call | flops 352321536 | bytes 2293760 | tf_op jit(solution)/shard_map/finish/pallas_call | solution.py:373
Async XLA Ops:
  36.1 19.6 %all-to-all-start = ((bf16[16,24,512]{2,1,0:T(8,128)(2,1)}), bf16[16,24,512]{2,1,0:T(8,128)(2,1)S(1)}, u32[]{:S(2)}, u32[]{:S(2)}) async-start(bf16[16,24,512]{2,1,0:T(8,128)(2,1)} %bitcast.18), calls=%async_computation | async-start | bytes 786432 | tf_op jit(solution)/shard_map/all_to_all | solution.py:386
  55.7 0.8 copy-start
  67.2 17.9 %all-to-all-start.2 = ((bf16[16,24,256]{2,1,0:T(8,128)(2,1)}), bf16[16,24,256]{2,1,0:T(8,128)(2,1)S(1)}, u32[]{:S(2)}, u32[]{:S(2)}) async-start(bf16[16,24,256]{2,1,0:T(8,128)(2,1)} %bitcast.19), calls=%async_computation.2 | async-start | bytes 393216 | tf_op jit(solution)/shard_map/all_to_all | solution.py:386
  85.1 36.2 %copy-start.1 = (bf16[16,24,256]{2,1,0:T(8,128)(2,1)}, bf16[16,24,256]{2,1,0:T(8,128)(2,1)S(1)}, u32[]{:S(2)}) copy-start(bf16[16,24,256]{2,1,0:T(8,128)(2,1)S(1)} %all-to-all-done.2) | copy-start | bytes 589828

commit v3 on v2

--- a/solution.py
+++ b/solution.py
@@ -13,8 +13,8 @@
 FOLD = 4
 STEP = 512
 DEPTH = 8
-DISPATCH = (1280, 512)
-RETURN = (256, 1536)
+DISPATCH = (1024, 768)
+BACK_COLUMNS = 512
 VMEM_BYTES = 56 * 1024 * 1024
 
 
@@ -158,14 +158,15 @@
 
 class Stream:
     def __init__(self, buffer, sems, tiles):
+        self.buffer = buffer
         self.depth = buffer.shape[0]
-        self.buffer = buffer
+        self.parts = []
         self.copies = []
         for n, tile in enumerate(tiles):
             slot = n % self.depth
-            self.copies.append(
-                pltpu.make_async_copy(tile, buffer.at[slot], sems.at[slot])
-            )
+            part = buffer.at[slot, pl.ds(0, tile.shape[0]), pl.ds(0, tile.shape[1])]
+            self.parts.append(part)
+            self.copies.append(pltpu.make_async_copy(tile, part, sems.at[slot]))
         self.begun = 0
 
     def ahead(self, upto):
@@ -174,9 +175,8 @@
             self.begun += 1
 
     def take(self, n):
-        self.ahead(n + 1)
         self.copies[n].wait()
-        return self.buffer[n % self.depth]
+        return self.parts[n][...]
 
     def free(self, n):
         self.ahead(n + 1 + self.depth)
@@ -190,22 +190,16 @@
         x_ref[:, q * width : (q + 1) * width] = value[q * rows : (q + 1) * rows]
 
 
-def refold(o_ref, order_ref, block_ref):
-    width = block_ref.shape[1]
-    value = jnp.concatenate(
-        [o_ref[:, q * width : (q + 1) * width] for q in range(FOLD)], axis=0
-    )
-    block_ref[...] = jnp.dot(
-        order_ref[...], value, preferred_element_type=jnp.float32
-    ).astype(jnp.bfloat16)
-
-
-def project(x_ref, tiles, accg_ref, accu_ref, fresh):
+def project(x_ref, tiles, totals, given):
     for n in range(x_ref.shape[1] // STEP):
         x = x_ref[:, n * STEP : (n + 1) * STEP]
-        for m, acc in enumerate((accg_ref, accu_ref)):
+        for m, total in enumerate(totals):
             value = jnp.dot(x, tiles.take(2 * n + m), preferred_element_type=jnp.float32)
-            acc[...] = value if fresh and n == 0 else acc[...] + value
+            if n > 0:
+                value = total[...] + value
+            elif given is not None:
+                value = given[m][...] + value
+            total[...] = value
             tiles.free(2 * n + m)
 
 
@@ -215,15 +209,11 @@
     ]
 
 
-def out_tiles(wd_ref, start, count):
-    return [wd_ref.at[0, :, pl.ds(start + n * STEP, STEP)] for n in range(count)]
-
-
 def first_kernel(start, order_ref, block_ref, wg_ref, wu_ref, accg_ref, accu_ref, x_ref, w_ref, sem):
     tiles = Stream(w_ref, sem, in_tiles(wg_ref, wu_ref, start, x_ref.shape[1] // STEP))
     tiles.ahead(tiles.depth)
     unfold(block_ref, order_ref, x_ref)
-    project(x_ref, tiles, accg_ref, accu_ref, True)
+    project(x_ref, tiles, (accg_ref, accu_ref), None)
 
 
 def first_part(order, block, gate_weight, up_weight, start):
@@ -246,15 +236,7 @@
     )(order, block, gate_weight, up_weight)
 
 
-def down(hidden_ref, tiles, o_ref):
-    for n in range(o_ref.shape[1] // STEP):
-        o_ref[:, n * STEP : (n + 1) * STEP] = jnp.dot(
-            hidden_ref[...], tiles.take(n), preferred_element_type=jnp.float32
-        ).astype(jnp.bfloat16)
-        tiles.free(n)
-
-
-def middle_kernel(
+def second_kernel(
     start,
     order_ref,
     back_ref,
@@ -264,86 +246,65 @@
     wg_ref,
     wu_ref,
     wd_ref,
-    hidden_ref,
     out_ref,
     x_ref,
     accg_ref,
     accu_ref,
-    o_ref,
+    hidden_ref,
     w_ref,
     d_ref,
     sem,
     dsem,
 ):
+    width = out_ref.shape[1]
+    spans = [(j, min(BACK_COLUMNS, width - j)) for j in range(0, width, BACK_COLUMNS)]
     tiles = Stream(w_ref, sem, in_tiles(wg_ref, wu_ref, start, x_ref.shape[1] // STEP))
-    outs = Stream(d_ref, dsem, out_tiles(wd_ref, 0, o_ref.shape[1] // STEP))
+    outs = Stream(
+        d_ref,
+        dsem,
+        [wd_ref.at[0, :, pl.ds(q * width + j, w)] for j, w in spans for q in range(FOLD)],
+    )
     tiles.ahead(tiles.depth)
     outs.ahead(outs.depth)
     unfold(block_ref, order_ref, x_ref)
-    accg_ref[...] = ing_ref[...]
-    accu_ref[...] = inu_ref[...]
-    project(x_ref, tiles, accg_ref, accu_ref, False)
+    project(x_ref, tiles, (accg_ref, accu_ref), (ing_ref, inu_ref))
     gate_val = accg_ref[...]
     hidden_ref[...] = (gate_val / (1.0 + jnp.exp(-gate_val)) * accu_ref[...]).astype(jnp.bfloat16)
-    down(hidden_ref, outs, o_ref)
-    refold(o_ref, back_ref, out_ref)
-
-
-def middle_part(order, back, block, accs, gate_weight, up_weight, down_weight, start):
+    for i, (j, w) in enumerate(spans):
+        values = []
+        for n in range(i * FOLD, (i + 1) * FOLD):
+            value = jnp.dot(hidden_ref[...], outs.take(n), preferred_element_type=jnp.float32)
+            values.append(value.astype(jnp.bfloat16))
+            outs.free(n)
+        out_ref[:, j : j + w] = jnp.dot(
+            back_ref[...], jnp.concatenate(values, axis=0), preferred_element_type=jnp.float32
+        ).astype(jnp.bfloat16)
+
+
+def second_part(order, back, block, accs, gate_weight, up_weight, down_weight, start):
     rows = block.shape[0] // FOLD
-    model, hidden = FOLD * block.shape[1], gate_weight.shape[2]
-    model_out = FOLD * RETURN[0]
-    out_depth = min(DEPTH // 2, model_out // STEP)
+    model, hidden, whole = FOLD * block.shape[1], down_weight.shape[1], down_weight.shape[2]
     return pl.pallas_call(
-        functools.partial(middle_kernel, start),
-        out_shape=[
-            jax.ShapeDtypeStruct((rows, hidden), jnp.bfloat16),
-            jax.ShapeDtypeStruct((block.shape[0], RETURN[0]), jnp.bfloat16),
-        ],
+        functools.partial(second_kernel, start),
+        out_shape=jax.ShapeDtypeStruct((block.shape[0], whole // FOLD), jnp.bfloat16),
         in_specs=[VMEM] * 5 + [HBM] * 3,
-        out_specs=[VMEM, VMEM],
+        out_specs=VMEM,
         scratch_shapes=[
             pltpu.VMEM((rows, model), jnp.bfloat16),
             pltpu.VMEM((rows, hidden), jnp.float32),
             pltpu.VMEM((rows, hidden), jnp.float32),
-            pltpu.VMEM((rows, model_out), jnp.bfloat16),
-            pltpu.VMEM((DEPTH, STEP, hidden), jnp.bfloat16),
-            pltpu.VMEM((out_depth, hidden, STEP), jnp.bfloat16),
+            pltpu.VMEM((rows, hidden), jnp.bfloat16),
+            pltpu.VMEM((2 * model // STEP, STEP, hidden), jnp.bfloat16),
+            pltpu.VMEM((DEPTH, hidden, BACK_COLUMNS), jnp.bfloat16),
+            pltpu.SemaphoreType.DMA((2 * model // STEP,)),
             pltpu.SemaphoreType.DMA((DEPTH,)),
-            pltpu.SemaphoreType.DMA((out_depth,)),
         ],
         compiler_params=params(),
         cost_estimate=cost(
-            2 * rows * (2 * model + model_out) * hidden, 2 * (2 * model + model_out) * hidden
+            2 * rows * (2 * model + whole) * hidden, 2 * (2 * model + whole) * hidden
         ),
-        name="middle_part",
+        name="second_part",
     )(order, back, block, *accs, gate_weight, up_weight, down_weight)
-
-
-def last_kernel(start, back_ref, hidden_ref, wd_ref, out_ref, o_ref, d_ref, dsem):
-    outs = Stream(d_ref, dsem, out_tiles(wd_ref, start, o_ref.shape[1] // STEP))
-    outs.ahead(outs.depth)
-    down(hidden_ref, outs, o_ref)
-    refold(o_ref, back_ref, out_ref)
-
-
-def last_part(back, hidden, down_weight, start, width):
-    rows, inner = hidden.shape
-    model_out = FOLD * width
-    return pl.pallas_call(
-        functools.partial(last_kernel, start),
-        out_shape=jax.ShapeDtypeStruct((FOLD * rows, width), jnp.bfloat16),
-        in_specs=[VMEM, VMEM, HBM],
-        out_specs=VMEM,
-        scratch_shapes=[
-            pltpu.VMEM((rows, model_out), jnp.bfloat16),
-            pltpu.VMEM((DEPTH, inner, STEP), jnp.bfloat16),
-            pltpu.SemaphoreType.DMA((DEPTH,)),
-        ],
-        compiler_params=params(),
-        cost_estimate=cost(2 * rows * model_out * inner, 2 * model_out * inner),
-        name="last_part",
-    )(back, hidden, down_weight)
 
 
 def column(row):
@@ -401,15 +362,13 @@
     order = jnp.asarray(matrix, jnp.bfloat16)
     back = jnp.asarray(matrix.T, jnp.bfloat16)
     base, *pieces = dispatch(placement, experts, replicas, tokens, slots)
-    arrived = [swap(piece, slots) for piece in pieces]
-    accs = first_part(order, arrived[0], gate_weight, up_weight, 0)
-    hidden, back_first = middle_part(
-        order, back, arrived[1], accs, gate_weight, up_weight, down_weight, FOLD * DISPATCH[0]
-    )
-    returned = [swap(back_first, slots)]
-    back_second = last_part(back, hidden, down_weight, FOLD * RETURN[0], RETURN[1])
-    returned.append(swap(back_second, slots))
-    return finish(base, gates, returned)
+    early = swap(pieces[0], slots)
+    late, _ = lax.optimization_barrier((pieces[1], early))
+    late = swap(late, slots)
+    accs = first_part(order, early, gate_weight, up_weight, 0)
+    start = FOLD * DISPATCH[0]
+    results = second_part(order, back, late, accs, gate_weight, up_weight, down_weight, start)
+    return finish(base, gates, [swap(results, slots)])
 
 
 def solution(mesh):

time: 125 us -> 121 us (0.968)
  starting transfers between devices: 9.49 us -> 3.58 us
  waiting for transfers between devices: 0.01 us -> 3.56 us
  blocking collectives: 69.4 us -> 67.6 us
    all_to_all x2 -> x1, starting transfers between devices: 9.49 us -> 3.58 us  [swap(): lax.all_to_all(block.reshape(slots, rows // slots, width), ('node', 'loca...]
    all_to_all x2 -> x1, waiting for transfers between devices: 0.01 us -> 3.56 us  [swap(): lax.all_to_all(block.reshape(slots, rows // slots, width), ('node', 'loca...]
    pallas_call x1, Pallas kernels: 16 us -> 13.5 us  [first_part(): pl.pallas_call(functools.partial(first_kernel, start), out_shape=[acc, ac...]
    pallas_call x2 -> x1, Pallas kernels: 22.7 us -> 24.5 us  [second_part(): pl.pallas_call(functools.partial(second_kernel, start), out_shape=jax.Sha...]
    all_to_all x2, blocking collectives: 69.4 us -> 67.6 us  [swap(): lax.all_to_all(block.reshape(slots, rows // slots, width), ('node', 'loca...]
  transfers between devices with their start and end apart: 2 -> 1, of which waited for: 0 -> 1; matrix products, arithmetic and copies ran while one was open for 0% -> 0% of each run, Pallas kernels for 22% -> 11%
where the time goes in v3:
time: 121 us; the launch traced here: 120 us
  blocking collectives  67.6 us (56%)
  Pallas kernels  44.5 us (37%)
  starting transfers between devices  3.58 us (3%)
  waiting for transfers between devices  3.56 us (3%)
    all_to_all x2, blocking collectives, swap(): lax.all_to_all(block.reshape(slots, rows // slots, width), ('node', 'loca...  67.6 us
    pallas_call x1, Pallas kernels, second_part(): pl.pallas_call(functools.partial(second_kernel, start), out_shape=jax.Sha...  24.5 us
    pallas_call x1, Pallas kernels, first_part(): pl.pallas_call(functools.partial(first_kernel, start), out_shape=[acc, ac...  13.5 us
    all_to_all x1, starting transfers between devices, swap(): lax.all_to_all(block.reshape(slots, rows // slots, width), ('node', 'loca...  3.58 us
    all_to_all x1, waiting for transfers between devices, swap(): lax.all_to_all(block.reshape(slots, rows // slots, width), ('node', 'loca...  3.56 us
    pallas_call x1, Pallas kernels, finish(): pl.pallas_call(finish_kernel, out_shape=jax.ShapeDtypeStruct((tok, model)...  3.43 us
    pallas_call x1, Pallas kernels, dispatch(): pl.pallas_call(functools.partial(dispatch_kernel, DISPATCH), out_shape=ou...  2.94 us
  transfers between devices with their start and end apart: 1, of which 1 were waited for; matrix products, arithmetic and copies ran while one was open for 0% of the time, Pallas kernels for 11%

profile of v3, /device:TPU:0, one launch (start us, length us, event | category | flops | bytes accessed | tf_op | source)
XLA Modules:
  0.0 120.1 jit_solution(14130803662840059567)
XLA Ops:
  0.0 2.9 %dispatch.1 = (s32[1,64]{1,0:T(1,128)}, bf16[384,1024]{1,0:T(8,128)(2,1)}, bf16[384,768]{1,0:T(8,128)(2,1)}) custom-call(s32[2,12]{1,0:T(2,128)} %bitcast.17, s32[1,64]{1,0:T(1,128)} %bitcast.18, s32[1,64]{1,0:T(1,128)} %bitcast.19, bf16[64,7168]{1,0:T(8,128)(2,1)} %tokens_ref.1), custom_call_target="tpu_custom_call" | custom-call | flops 352321536 | bytes 2293760 | tf_op jit(solution)/shard_map/dispatch/pallas_call | solution.py:148
  2.9 29.1 %all_to_all.15 = bf16[16,24,1024]{2,1,0:T(8,128)(2,1)} all-to-all(bf16[16,24,1024]{2,1,0:T(8,128)(2,1)} %bitcast.14), channel_id=1, replica_groups=mesh['parts'=2,'node'=2,'local'=8] {'node','local'}, dimensions={0} | all-to-all | bytes 1572864 | tf_op jit(solution)/shard_map/all_to_all | solution.py:347
  32.0 3.6 %all-to-all-start.1 = ((bf16[16,24,768]{2,1,0:T(8,128)(2,1)}), bf16[16,24,768]{2,1,0:T(8,128)(2,1)S(1)}, u32[]{:S(2)}, u32[]{:S(2)}) async-start(bf16[16,24,768]{2,1,0:T(8,128)(2,1)} %bitcast.15), calls=%async_computation.1 | async-start | bytes 1179648 | tf_op jit(solution)/shard_map/all_to_all | solution.py:347
  35.6 13.5 %first_part.1 = (f32[96,2048]{1,0:T(8,128)}, f32[96,2048]{1,0:T(8,128)}) custom-call(bf16[384,384]{1,0:T(8,128)(2,1)} %constant.4.clone.order_ref, bf16[384,1024]{1,0:T(8,128)(2,1)} %bitcast.12, bf16[1,7168,2048]{2,1,0:T(8,128)(2,1)} %wg_ref.3, bf16[1,7168,2048]{2,1,0:T(8,128)(2,1)} %wu_ref.3), custom_call_target="tpu_custom_call" | custom-call | flops 3221225472 | bytes 33554432 | tf_op jit(solution)/shard_map/first_part/pallas_call | solution.py:223
  49.1 3.6 %all-to-all-done.1 = bf16[16,24,768]{2,1,0:T(8,128)(2,1)S(1)} async-done(((bf16[16,24,768]{2,1,0:T(8,128)(2,1)}), bf16[16,24,768]{2,1,0:T(8,128)(2,1)S(1)}, u32[]{:S(2)}, u32[]{:S(2)}) %all-to-all-start.1) | async-done | bytes 589856 | tf_op jit(solution)/shard_map/all_to_all | solution.py:347
  52.7 0.0 copy-start
  52.7 0.8 copy-done
  53.5 24.5 %second_part.1 = bf16[384,1792]{1,0:T(8,128)(2,1)} custom-call(bf16[384,384]{1,0:T(8,128)(2,1)} %constant.4.clone.order_ref, bf16[384,384]{1,0:T(8,128)(2,1)} %constant.5.clone.back_ref, bf16[384,768]{1,0:T(8,128)(2,1)} %bitcast.13, f32[96,2048]{1,0:T(8,128)} %get-tuple-element.15.ing_ref, f32[96,2048]{1,0:T(8,128)} %get-tuple-element.16.inu_ref, ...), custom_call_target="tpu_custom_call" | custom-call | flops 5234491392 | bytes 54525952 | tf_op jit(solution)/shard_map/second_part/pallas_call | solution.py:287
  78.1 38.6 %all_to_all.16 = bf16[16,24,1792]{2,1,0:T(8,128)(2,1)} all-to-all(bf16[16,24,1792]{2,1,0:T(8,128)(2,1)} %bitcast.10), channel_id=1, replica_groups=mesh['parts'=2,'node'=2,'local'=8] {'node','local'}, dimensions={0} | all-to-all | bytes 2752512 | tf_op jit(solution)/shard_map/all_to_all | solution.py:347
  116.6 3.4 %finish.1 = bf16[64,7168]{1,0:T(8,128)(2,1)} custom-call(s32[1,64]{1,0:T(1,128)} %get-tuple-element.11.base_ref, f32[1,64]{1,0:T(1,128)} %bitcast.16, bf16[384,1792]{1,0:T(8,128)(2,1)} %bitcast.11), custom_call_target="tpu_custom_call" | custom-call | flops 352321536 | bytes 2293760 | tf_op jit(solution)/shard_map/finish/pallas_call | solution.py:334
Async XLA Ops:
  32.0 20.7 %all-to-all-start.1 = ((bf16[16,24,768]{2,1,0:T(8,128)(2,1)}), bf16[16,24,768]{2,1,0:T(8,128)(2,1)S(1)}, u32[]{:S(2)}, u32[]{:S(2)}) async-start(bf16[16,24,768]{2,1,0:T(8,128)(2,1)} %bitcast.15), calls=%async_computation.1 | async-start | bytes 1179648 | tf_op jit(solution)/shard_map/all_to_all | solution.py:347
  52.7 0.8 copy-start

commit v4 on v3

v4 whole, which is shorter than its diff:
```python
import functools

import jax
import jax.numpy as jnp
import numpy as np
from jax import lax
from jax.experimental import pallas as pl
from jax.experimental.pallas import tpu as pltpu
from jax.sharding import PartitionSpec as P

FF = 2048
CAP = 6
FOLD = 4
STEP = 512
FLIGHT = 4
DEPTH = 6
HOPS = (1, 2, 4, 6, 5, 7, 3)
LAG = 3
DISPATCH = (896, 896)
BACK_COLUMNS = 512
VMEM_BYTES = 56 * 1024 * 1024


def route_tables(experts, replicas, gates, placement, slot_count, capacity):
    expert_hit = (
        experts[:, :, None] == jnp.arange(placement.shape[0], dtype=jnp.int32)[None, None, :]
    )
    replica_hit = (
        replicas[:, :, None] == jnp.arange(placement.shape[1], dtype=jnp.int32)[None, None, :]
    )
    joined = expert_hit[:, :, :, None] & replica_hit[:, :, None, :]
    slot_ids = jnp.sum(jnp.where(joined, placement[None, None, :, :], 0), axis=(2, 3))
    flat_slots = slot_ids.reshape(-1)
    slot_hit = (flat_slots[:, None] == jnp.arange(slot_count, dtype=jnp.int32)[None, :]).astype(
        jnp.int32
    )
    before = jnp.cumsum(slot_hit, axis=0) - slot_hit
    rank = jnp.sum(slot_hit * before, axis=1)
    position = (flat_slots * capacity + rank).reshape(slot_ids.shape)
    grid = position[:, :, None] == jnp.arange(slot_count * capacity, dtype=jnp.int32)[None, None, :]
    scatter = jnp.any(grid, axis=1).T
    zero_gate = jnp.zeros_like(gates)[:, :, None]
    combine = jnp.sum(jnp.where(grid, gates[:, :, None], zero_gate), axis=1)
    return (scatter, combine)


def per_device_general(
    tokens, experts, replicas, gates, placement, gate_weight, up_weight, down_weight
):
    model_width = tokens.shape[1]
    hidden_dev = gate_weight.shape[2]
    group_size = FF // hidden_dev
    devices_all = lax.axis_size(("node", "local"))
    slot_count = devices_all // group_size
    capacity = CAP
    scatter, combine = route_tables(experts, replicas, gates, placement, slot_count, capacity)
    outgoing = jnp.dot(
        scatter.astype(jnp.bfloat16), tokens, preferred_element_type=jnp.float32
    ).astype(jnp.bfloat16)
    outgoing = outgoing.reshape(slot_count, capacity, model_width)
    sending = jnp.repeat(outgoing, group_size, axis=0)
    arrived = lax.all_to_all(sending, ("node", "local"), split_axis=0, concat_axis=0, tiled=True)
    row_block = arrived.reshape(-1, model_width)
    gate_val = jnp.dot(row_block, gate_weight[0], preferred_element_type=jnp.float32)
    up_val = jnp.dot(row_block, up_weight[0], preferred_element_type=jnp.float32)
    hidden = (jax.nn.silu(gate_val) * up_val).astype(jnp.bfloat16)
    partial_value = (
        jnp.dot(hidden, down_weight[0], preferred_element_type=jnp.float32)
        .astype(jnp.bfloat16)
        .reshape(arrived.shape)
    )
    returned = lax.all_to_all(
        partial_value, ("node", "local"), split_axis=0, concat_axis=0, tiled=True
    )
    summed = jnp.sum(
        returned.reshape(slot_count, group_size, capacity, model_width).astype(jnp.float32), axis=1
    )
    mixed = jnp.dot(
        combine,
        summed.reshape(slot_count * capacity, model_width),
        precision=lax.Precision.HIGHEST,
        preferred_element_type=jnp.float32,
    )
    return mixed.astype(jnp.bfloat16)


def params(size=VMEM_BYTES):
    return pltpu.CompilerParams(vmem_limit_bytes=size)


VMEM = pl.BlockSpec(memory_space=pltpu.VMEM)
SMEM = pl.BlockSpec(memory_space=pltpu.SMEM)
HBM = pl.BlockSpec(memory_space=pl.ANY)


def cost(flops, size):
    return pl.CostEstimate(flops=int(flops), bytes_accessed=int(size), transcendentals=0)


def fold_matrix(groups):
    g, q, c = np.meshgrid(np.arange(groups), np.arange(FOLD), np.arange(CAP), indexing="ij")
    size = groups * FOLD * CAP
    matrix = np.zeros((size, size), np.float32)
    matrix[
        (q * groups * CAP + g * CAP + c).ravel(), (g * FOLD * CAP + q * CAP + c).ravel()
    ] = 1.0
    return matrix


def fold_table(n_local):
    q, k, b, c = np.meshgrid(
        np.arange(FOLD), np.arange(n_local), np.arange(2), np.arange(CAP), indexing="ij"
    )
    table = np.zeros((8, q.size), np.int32)
    table[0], table[1], table[2] = k.ravel(), b.ravel(), (q * CAP + c).ravel()
    return table


def dispatch_kernel(n_local, place_ref, own_pick, mate_pick, own_ref, mate_ref, spot_ref, *blocks):
    tok = own_ref.shape[0]
    both = 2 * tok
    node, local = lax.axis_index("node"), lax.axis_index("local")
    slots = 2 * n_local
    pick = jnp.concatenate([own_pick[...], mate_pick[...]], axis=1)
    slot = jnp.zeros((1, both), jnp.int32)
    columns = place_ref.shape[0]
    for e in range(place_ref.shape[1]):
        for r in range(columns):
            slot = jnp.where(pick == e * columns + r, place_ref[r, e], slot)
    hit = lax.broadcasted_iota(jnp.int32, (slots, both), 0) == slot
    early = lax.broadcasted_iota(jnp.int32, (both, both), 0)
    late = lax.broadcasted_iota(jnp.int32, (both, both), 1)
    earlier = (early < late) & ((early >= tok) == (late >= tok))
    before = jnp.dot(
        hit.astype(jnp.bfloat16), earlier.astype(jnp.bfloat16), preferred_element_type=jnp.float32
    )
    rank = jnp.sum(jnp.where(hit, before, 0.0), axis=0, keepdims=True).astype(jnp.int32)
    there = slot - node * n_local
    hop = there ^ local
    second = (lax.broadcasted_iota(jnp.int32, (1, both), 1) >= tok).astype(jnp.int32)
    base = jnp.where(
        (there >= 0) & (there < n_local), (hop * 2 + second) * (FOLD * CAP) + rank, -FOLD * CAP
    )
    spot_ref[...] = (slot * (FOLD * CAP) + rank)[:, :tok]
    size = 2 * FOLD * CAP
    row = lax.broadcasted_iota(jnp.int32, (n_local * size, both), 0)
    select = jnp.concatenate(
        [(row == base + q * CAP).astype(jnp.bfloat16) for q in range(FOLD)], axis=1
    )
    start = 0
    for piece, width in enumerate(DISPATCH):
        folded = jnp.concatenate(
            [
                ref[:, start + q * width : start + (q + 1) * width]
                for q in range(FOLD)
                for ref in (own_ref, mate_ref)
            ],
            axis=0,
        )
        value = jnp.dot(select, folded, preferred_element_type=jnp.float32).astype(jnp.bfloat16)
        for hop_id in range(n_local):
            blocks[piece * n_local + hop_id][...] = value[hop_id * size : (hop_id + 1) * size]
        start += FOLD * width


def dispatch(placement, own_pick, mate_pick, own, mate, n_local):
    tok, model = own.shape
    size = 2 * FOLD * CAP
    out_shape = [jax.ShapeDtypeStruct((1, tok), jnp.int32)] + [
        jax.ShapeDtypeStruct((size, width), jnp.bfloat16)
        for width in DISPATCH
        for _ in range(n_local)
    ]
    outs = pl.pallas_call(
        functools.partial(dispatch_kernel, n_local),
        out_shape=out_shape,
        in_specs=[SMEM, VMEM, VMEM, VMEM, VMEM],
        out_specs=[VMEM] * len(out_shape),
        compiler_params=params(),
        cost_estimate=cost(4 * n_local * size * tok * model, 10 * tok * model),
        name="dispatch",
    )(placement.T, own_pick, mate_pick, own, mate)
    return outs[0], [outs[1 + i * n_local : 1 + (i + 1) * n_local] for i in range(len(DISPATCH))]


class Stream:
    def __init__(self, *kinds):
        self.parts = []
        self.copies = []
        for buffer, sems, tiles in kinds:
            for n, tile in enumerate(tiles):
                slot = n % buffer.shape[0]
                part = buffer.at[slot, pl.ds(0, tile.shape[0]), pl.ds(0, tile.shape[1])]
                self.parts.append(part)
                self.copies.append(pltpu.make_async_copy(tile, part, sems.at[slot]))
        self.taken = 0
        for copy in self.copies[:FLIGHT]:
            copy.start()

    def take(self):
        n = self.taken
        self.copies[n].wait()
        if n + FLIGHT < len(self.copies):
            self.copies[n + FLIGHT].start()
        self.taken += 1
        return self.parts[n][...]


def unfold(blocks, order_ref, x_ref):
    rows, width = x_ref.shape[0], blocks[0].shape[1]
    folded = jnp.concatenate([b[...] for b in blocks], axis=0)
    value = jnp.dot(order_ref[...], folded, preferred_element_type=jnp.float32)
    value = value.astype(jnp.bfloat16)
    for q in range(FOLD):
        x_ref[:, q * width : (q + 1) * width] = value[q * rows : (q + 1) * rows]


def project(x_ref, tiles, totals, given):
    for n in range(x_ref.shape[1] // STEP):
        x = x_ref[:, n * STEP : (n + 1) * STEP]
        for m, total in enumerate(totals):
            value = jnp.dot(x, tiles.take(), preferred_element_type=jnp.float32)
            if n > 0:
                value = total[...] + value
            elif given is not None:
                value = given[m][...] + value
            total[...] = value


def in_tiles(wg_ref, wu_ref, start, count):
    return [
        w.at[0, pl.ds(start + n * STEP, STEP)] for n in range(count) for w in (wg_ref, wu_ref)
    ]


def first_kernel(n_local, start, order_ref, *refs):
    blocks = refs[:n_local]
    wg_ref, wu_ref, accg_ref, accu_ref, x_ref, w_ref, sem = refs[n_local:]
    tiles = Stream((w_ref, sem, in_tiles(wg_ref, wu_ref, start, x_ref.shape[1] // STEP)))
    unfold(blocks, order_ref, x_ref)
    project(x_ref, tiles, (accg_ref, accu_ref), None)


def first_part(order, blocks, gate_weight, up_weight, start):
    n_local = len(blocks)
    rows = 2 * n_local * CAP
    model, hidden = FOLD * blocks[0].shape[1], gate_weight.shape[2]
    acc = jax.ShapeDtypeStruct((rows, hidden), jnp.float32)
    return pl.pallas_call(
        functools.partial(first_kernel, n_local, start),
        out_shape=[acc, acc],
        in_specs=[VMEM] * (1 + n_local) + [HBM] * 2,
        out_specs=[VMEM, VMEM],
        scratch_shapes=[
            pltpu.VMEM((rows, model), jnp.bfloat16),
            pltpu.VMEM((DEPTH, STEP, hidden), jnp.bfloat16),
            pltpu.SemaphoreType.DMA((DEPTH,)),
        ],
        compiler_params=params(),
        cost_estimate=cost(4 * rows * model * hidden, 4 * model * hidden),
        name="first_part",
    )(order, *blocks, gate_weight, up_weight)


def second_kernel(n_local, start, order_ref, table_ref, *refs):
    blocks, refs = refs[:n_local], refs[n_local:]
    ing_ref, inu_ref, wg_ref, wu_ref, wd_ref, out_ref = refs[:6]
    x_ref, accg_ref, accu_ref, hidden_ref, w_ref, d_ref, sem, dsem = refs[6:]
    width = out_ref.shape[1]
    spans = [(j, min(BACK_COLUMNS, width - j)) for j in range(0, width, BACK_COLUMNS)]
    out_tiles = [wd_ref.at[0, :, pl.ds(q * width + j, w)] for j, w in spans for q in range(FOLD)]
    tiles = Stream(
        (w_ref, sem, in_tiles(wg_ref, wu_ref, start, x_ref.shape[1] // STEP)),
        (d_ref, dsem, out_tiles),
    )
    node, local = lax.axis_index("node"), lax.axis_index("local")
    device = (table_ref[1:2, :] ^ node) * n_local + (table_ref[0:1, :] ^ local)
    target = device * (FOLD * CAP) + table_ref[2:3, :]
    size = target.shape[1]
    back = (lax.broadcasted_iota(jnp.int32, (size, size), 0) == target).astype(jnp.bfloat16)
    unfold(blocks, order_ref, x_ref)
    project(x_ref, tiles, (accg_ref, accu_ref), (ing_ref, inu_ref))
    gate_val = accg_ref[...]
    hidden_ref[...] = (gate_val / (1.0 + jnp.exp(-gate_val)) * accu_ref[...]).astype(jnp.bfloat16)
    for j, w in spans:
        values = []
        for _ in range(FOLD):
            value = jnp.dot(hidden_ref[...], tiles.take(), preferred_element_type=jnp.float32)
            values.append(value.astype(jnp.bfloat16))
        out_ref[:, j : j + w] = jnp.dot(
            back, jnp.concatenate(values, axis=0), preferred_element_type=jnp.float32
        ).astype(jnp.bfloat16)


def second_part(order, table, blocks, accs, gate_weight, up_weight, down_weight, start):
    n_local = len(blocks)
    rows = 2 * n_local * CAP
    model, hidden, whole = FOLD * blocks[0].shape[1], down_weight.shape[1], down_weight.shape[2]
    return pl.pallas_call(
        functools.partial(second_kernel, n_local, start),
        out_shape=jax.ShapeDtypeStruct((rows * FOLD, whole // FOLD), jnp.bfloat16),
        in_specs=[VMEM] * (4 + n_local) + [HBM] * 3,
        out_specs=VMEM,
        scratch_shapes=[
            pltpu.VMEM((rows, model), jnp.bfloat16),
            pltpu.VMEM((rows, hidden), jnp.float32),
            pltpu.VMEM((rows, hidden), jnp.float32),
            pltpu.VMEM((rows, hidden), jnp.bfloat16),
            pltpu.VMEM((DEPTH, STEP, hidden), jnp.bfloat16),
            pltpu.VMEM((DEPTH, hidden, BACK_COLUMNS), jnp.bfloat16),
            pltpu.SemaphoreType.DMA((DEPTH,)),
            pltpu.SemaphoreType.DMA((DEPTH,)),
        ],
        compiler_params=params(),
        cost_estimate=cost(
            2 * rows * (2 * model + whole) * hidden, 2 * (2 * model + whole) * hidden
        ),
        name="second_part",
    )(order, table, *blocks, *accs, gate_weight, up_weight, down_weight)


def column(row):
    n = row.shape[1]
    eye = lax.broadcasted_iota(jnp.int32, (n, n), 0) == lax.broadcasted_iota(jnp.int32, (n, n), 1)
    return jnp.sum(jnp.where(eye, row, jnp.zeros_like(row)), axis=1, keepdims=True)


def finish_kernel(base_ref, gates_ref, *refs):
    pieces, out_ref = refs[:-1], refs[-1]
    base = column(base_ref[...])
    gate = column(gates_ref[...])
    lane = lax.broadcasted_iota(jnp.int32, (base.shape[0], pieces[0].shape[0]), 1)
    select = [(lane == base + q * CAP).astype(jnp.bfloat16) for q in range(FOLD)]
    start = 0
    for piece in pieces:
        width = piece.shape[1]
        for q in range(FOLD):
            value = jnp.dot(select[q], piece[...], preferred_element_type=jnp.float32)
            out_ref[:, start : start + width] = (gate * value).astype(jnp.bfloat16)
            start += width


def finish(base, gates, pieces):
    tok = base.shape[1]
    model = FOLD * sum(p.shape[1] for p in pieces)
    return pl.pallas_call(
        finish_kernel,
        out_shape=jax.ShapeDtypeStruct((tok, model), jnp.bfloat16),
        in_specs=[VMEM] * (2 + len(pieces)),
        out_specs=VMEM,
        compiler_params=params(8 * 1024 * 1024),
        cost_estimate=cost(2 * tok * model * 384, 5 * tok * model),
        name="finish",
    )(base, gates.reshape(1, tok), *pieces)


def swap(block, slots):
    rows, width = block.shape
    out = lax.all_to_all(
        block.reshape(slots, rows // slots, width),
        ("node", "local"),
        split_axis=0,
        concat_axis=0,
        tiled=True,
    )
    return out.reshape(rows, width)


def swap_hops(blocks, after=None):
    n_local = len(blocks)
    out = list(blocks)
    for n, hop in enumerate(HOPS):
        block = blocks[hop]
        if after is not None:
            earlier = after[HOPS[min(n + LAG, len(HOPS) - 1)]]
            block, _ = lax.optimization_barrier((block, earlier))
        out[hop] = lax.ppermute(block, "local", [(i, i ^ hop) for i in range(n_local)])
    return out


def swap_mate(value):
    return lax.ppermute(value, "node", [(0, 1), (1, 0)])


def per_device_folded(
    tokens, experts, replicas, gates, placement, gate_weight, up_weight, down_weight
):
    tok = tokens.shape[0]
    n_local = lax.axis_size("local")
    slots = 2 * n_local
    order = jnp.asarray(fold_matrix(slots), jnp.bfloat16)
    table = jnp.asarray(fold_table(n_local))
    mate = swap_mate(tokens)
    pick = (experts * placement.shape[1] + replicas).reshape(1, tok)
    spot, pieces = dispatch(placement, pick, swap_mate(pick), tokens, mate, n_local)
    early = swap_hops(pieces[0])
    late = swap_hops(pieces[1], early)
    accs = first_part(order, early, gate_weight, up_weight, 0)
    start = FOLD * DISPATCH[0]
    results = second_part(order, table, late, accs, gate_weight, up_weight, down_weight, start)
    return finish(spot, gates, [swap(results, slots)])


def solution(mesh):
    in_specs = (
        P(("parts", "node", "local"), None),
        P(("parts", "node", "local"), None),
        P(("parts", "node", "local"), None),
        P(("parts", "node", "local"), None),
        P(),
        P(("node", "local"), None, None),
        P(("node", "local"), None, None),
        P(("node", "local"), None, None),
    )
    out_specs = P(("parts", "node", "local"), None)

    def per_device(*args):
        folded = (
            mesh.shape["node"] == 2
            and mesh.shape["local"] == 8
            and args[1].shape[1] == 1
            and args[5].shape[2] == FF
            and args[0].shape[1] == FOLD * sum(DISPATCH)
        )
        return (per_device_folded if folded else per_device_general)(*args)

    return jax.shard_map(
        per_device, mesh=mesh, in_specs=in_specs, out_specs=out_specs, check_vma=False
    )
```

time: 121 us -> 113 us (0.934)
  blocking collectives: 67.6 us -> 39.7 us
  starting transfers between devices: 3.58 us -> 23.4 us
  Pallas kernels: 44.5 us -> 40.4 us
  waiting for transfers between devices: 3.56 us -> 6.1 us
    all_to_all x2 -> x1, blocking collectives: 67.6 us -> 39.7 us  [swap(): lax.all_to_all(block.reshape(slots, rows // slots, width), ('node', 'loca...]
    ppermute x0 -> x16, starting transfers between devices: none -> 23.4 us  [the longest x14 22.9 us: swap_hops(): lax.ppermute(block, 'local', [(i, i ^ hop) for i in range(n_local)])]
    ppermute x0 -> x16, waiting for transfers between devices: none -> 6.1 us  [the longest x14 4.53 us: swap_hops(): lax.ppermute(block, 'local', [(i, i ^ hop) for i in range(n_local)])]
    all_to_all x1 -> x0, starting transfers between devices: 3.58 us -> none  [swap(): lax.all_to_all(block.reshape(slots, rows // slots, width), ('node', 'loca...]
    all_to_all x1 -> x0, waiting for transfers between devices: 3.56 us -> none  [swap(): lax.all_to_all(block.reshape(slots, rows // slots, width), ('node', 'loca...]
    pallas_call x3, Pallas kernels: 41 us -> 38.4 us  [the longest x1 22.6 us: second_part(): pl.pallas_call(functools.partial(second_kernel, n_local, start), out_shap...]
    pallas_call x1, Pallas kernels: 3.43 us -> 2.08 us  [finish(): pl.pallas_call(finish_kernel, out_shape=jax.ShapeDtypeStruct((tok, model)...]
  transfers between devices with their start and end apart: 1 -> 16, of which waited for: 1 -> 3; matrix products, arithmetic and copies ran while one was open for 0% -> 1% of each run, Pallas kernels for 11% -> 11%
where the time goes in v4:
time: 113 us; the launch traced here: 112 us
  Pallas kernels  40.4 us (36%)
  blocking collectives  39.7 us (35%)
  starting transfers between devices  23.4 us (21%)
  waiting for transfers between devices  6.1 us (5%)
  local copies, waits for them, and re-layouts  1.66 us (1%)
    all_to_all x1, blocking collectives, swap(): lax.all_to_all(block.reshape(slots, rows // slots, width), ('node', 'loca...  39.7 us
    ppermute x14, starting transfers between devices, swap_hops(): lax.ppermute(block, 'local', [(i, i ^ hop) for i in range(n_local)])  22.9 us
    pallas_call x1, Pallas kernels, second_part(): pl.pallas_call(functools.partial(second_kernel, n_local, start), out_shap...  22.6 us
    pallas_call x1, Pallas kernels, first_part(): pl.pallas_call(functools.partial(first_kernel, n_local, start), out_shape...  12.3 us
    ppermute x14, waiting for transfers between devices, swap_hops(): lax.ppermute(block, 'local', [(i, i ^ hop) for i in range(n_local)])  4.53 us
    pallas_call x1, Pallas kernels, dispatch(): pl.pallas_call(functools.partial(dispatch_kernel, n_local), out_shape=out...  3.47 us
  transfers between devices with their start and end apart: 16, of which 3 were waited for; matrix products, arithmetic and copies ran while one was open for 1% of the time, Pallas kernels for 11%

profile of v4, /device:TPU:0, one launch (start us, length us, event | category | flops | bytes accessed | tf_op | source)
XLA Modules:
  0.0 112.3 jit_solution(6098167672564942271)
XLA Ops:
  0.0 0.5 collective-permute-start.1
  0.5 0.7 add_bitcast_fusion.own_pick
  1.2 1.4 %collective-permute-done.mate_pick = s32[1,64]{1,0:T(1,128)S(1)} collective-permute-done((s32[1,64]{1,0:T(1,128)S(1)}, s32[1,64]{1,0:T(1,128)S(1)}, u32[]{:S(2)}, u32[]{:S(2)}) %collective-permute-start) | collective-permute-done | bytes 288 | tf_op jit(solution)/shard_map/ppermute | solution.py:382
  2.6 0.2 collective-permute-done.1.mate_ref
  2.8 0.3 copy-done.18
  3.1 0.6 copy-done.16
  3.7 3.5 %dispatch.1 = (s32[1,64]{1,0:T(1,128)}, bf16[48,896]{1,0:T(8,128)(2,1)}, bf16[48,896]{1,0:T(8,128)(2,1)}, bf16[48,896]{1,0:T(8,128)(2,1)}, bf16[48,896]{1,0:T(8,...) custom-call(s32[2,12]{1,0:T(2,128)} %bitcast.9, ...), custom_call_target="tpu_custom_call" | custom-call | flops 704643072 | bytes 4587520 | tf_op jit(solution)/shard_map/dispatch/pallas_call | solution.py:174
  7.2 5.0 %collective-permute-start.2 = (bf16[48,896]{1,0:T(8,128)(2,1)}, bf16[48,896]{1,0:T(8,128)(2,1)S(1)}, u32[]{:S(2)}, u32[]{:S(2)}) collective-permute-start(bf16[48,896]{1,0:T(8,128)(2,1)} %get-tuple-element.34), channel_id=1, source_target_pairs={{0,6},{1,7},{2,4},{3,5},{4,2},{5,3},{6,0},{7,1},{8,14},{9,15},{10,... | collective-permute-start | bytes 258056 | tf_op jit(solution)/shard_map/ppermute | solution.py:377
  12.1 0.4 collective-permute-start.4
  12.5 1.2 %collective-permute-start.6 = (bf16[48,896]{1,0:T(8,128)(2,1)}, bf16[48,896]{1,0:T(8,128)(2,1)S(1)}, u32[]{:S(2)}, u32[]{:S(2)}) collective-permute-start(bf16[48,896]{1,0:T(8,128)(2,1)} %get-tuple-element.40), channel_id=1, source_target_pairs={{0,3},{1,2},{2,1},{3,0},{4,7},{5,6},{6,5},{7,4},{8,11},{9,10},{10,... | collective-permute-start | bytes 258056 | tf_op jit(solution)/shard_map/ppermute | solution.py:377
  13.7 4.7 %collective-permute-start.8 = (bf16[48,896]{1,0:T(8,128)(2,1)}, bf16[48,896]{1,0:T(8,128)(2,1)S(1)}, u32[]{:S(2)}, u32[]{:S(2)}) collective-permute-start(bf16[48,896]{1,0:T(8,128)(2,1)} %get-tuple-element.43), channel_id=1, source_target_pairs={{0,7},{1,6},{2,5},{3,4},{4,3},{5,2},{6,1},{7,0},{8,15},{9,14},{10,... | collective-permute-start | bytes 258056 | tf_op jit(solution)/shard_map/ppermute | solution.py:377
  18.3 0.5 collective-permute-start.13
  18.9 0.1 collective-permute-start.14
  19.0 4.5 %collective-permute-done.4.refs_5_ = bf16[48,896]{1,0:T(8,128)(2,1)S(1)} collective-permute-done((bf16[48,896]{1,0:T(8,128)(2,1)}, bf16[48,896]{1,0:T(8,128)(2,1)S(1)}, u32[]{:S(2)}, u32[]{:S(2)}) %collective-permute-start.4) | collective-permute-done | bytes 86048 | tf_op jit(solution)/shard_map/ppermute | solution.py:377
  23.6 2.8 %collective-permute-start.5 = (bf16[48,896]{1,0:T(8,128)(2,1)}, bf16[48,896]{1,0:T(8,128)(2,1)S(1)}, u32[]{:S(2)}, u32[]{:S(2)}) collective-permute-start(bf16[48,896]{1,0:T(8,128)(2,1)} %get-tuple-element.38), channel_id=1, source_target_pairs={{0,2},{1,3},{2,0},{3,1},{4,6},{5,7},{6,4},{7,5},{8,10},{9,11},{10,... | collective-permute-start | bytes 258056 | tf_op jit(solution)/shard_map/ppermute | solution.py:377
  26.4 1.5 %collective-permute-start.7 = (bf16[48,896]{1,0:T(8,128)(2,1)}, bf16[48,896]{1,0:T(8,128)(2,1)S(1)}, u32[]{:S(2)}, u32[]{:S(2)}) collective-permute-start(bf16[48,896]{1,0:T(8,128)(2,1)} %get-tuple-element.41), channel_id=1, source_target_pairs={{0,3},{1,2},{2,1},{3,0},{4,7},{5,6},{6,5},{7,4},{8,11},{9,10},{10,... | collective-permute-start | bytes 258056 | tf_op jit(solution)/shard_map/ppermute | solution.py:377
  27.9 3.3 %collective-permute-start.10 = (bf16[48,896]{1,0:T(8,128)(2,1)}, bf16[48,896]{1,0:T(8,128)(2,1)S(1)}, u32[]{:S(2)}, u32[]{:S(2)}) collective-permute-start(bf16[48,896]{1,0:T(8,128)(2,1)} %get-tuple-element.46), channel_id=1, source_target_pairs={{0,5},{1,4},{2,7},{3,6},{4,1},{5,0},{6,3},{7,2},{8,13},{9,12},{10,... | collective-permute-start | bytes 258056 | tf_op jit(solution)/shard_map/ppermute | solution.py:377
  31.2 0.8 collective-permute-start.11
  32.0 2.6 %collective-permute-start.12 = (bf16[48,896]{1,0:T(8,128)(2,1)}, bf16[48,896]{1,0:T(8,128)(2,1)S(1)}, u32[]{:S(2)}, u32[]{:S(2)}) collective-permute-start(bf16[48,896]{1,0:T(8,128)(2,1)} %get-tuple-element.50), channel_id=1, source_target_pairs={{0,7},{1,6},{2,5},{3,4},{4,3},{5,2},{6,1},{7,0},{8,15},{9,14},{10,... | collective-permute-start | bytes 258056 | tf_op jit(solution)/shard_map/ppermute | solution.py:377
  34.7 12.3 %first_part.1 = (f32[96,2048]{1,0:T(8,128)}, f32[96,2048]{1,0:T(8,128)}) custom-call(bf16[384,384]{1,0:T(8,128)(2,1)} %constant.6.clone.order_ref, bf16[48,896]{1,0:T(8,128)(2,1)} %get-tuple-element.51.refs_0_, bf16[48,896]{1,0:T(8,128)(2,1)} %copy-done.7, bf16[48,896]{1,0:T(8,128)(2,1)} %copy-done.9, bf16[48,896]{1,0:T(8,128)(2,1)} %copy-done.4, ...), custom_call_target="tpu_custom_call" | custom-call | flops 2818572288 | bytes 29360128 | tf_op jit(solution)/shard_map/first_part/pallas_call | solution.py:249
  47.2 0.6 copy-done.10
  47.9 22.6 %second_part.1 = bf16[384,1792]{1,0:T(8,128)(2,1)} custom-call(bf16[384,384]{1,0:T(8,128)(2,1)} %constant.6.clone.order_ref, s32[8,384]{1,0:T(8,128)} %constant.7.clone.table_ref, bf16[48,896]{1,0:T(8,128)(2,1)} %get-tuple-element.32.refs_0_, bf16[48,896]{1,0:T(8,128)(2,1)} %copy-done.5, bf16[48,896]{1,0:T(8,128)(2,1)} %copy-done.8, ...), custom_call_target="tpu_custom_call" | custom-call | flops 5637144576 | bytes 58720256 | tf_op jit(solution)/shard_map/second_part/pallas_call | solution.py:299
  70.5 39.7 %all_to_all.5 = bf16[16,24,1792]{2,1,0:T(8,128)(2,1)S(1)} all-to-all(bf16[16,24,1792]{2,1,0:T(8,128)(2,1)} %bitcast.8), channel_id=1, replica_groups=mesh['parts'=2,'node'=2,'local'=8] {'node','local'}, dimensions={0} | all-to-all | bytes 2752512 | tf_op jit(solution)/shard_map/all_to_all | solution.py:359
  110.2 2.1 %finish.1 = bf16[64,7168]{1,0:T(8,128)(2,1)} custom-call(s32[1,64]{1,0:T(1,128)S(1)} %copy-done.1, f32[1,64]{1,0:T(1,128)S(1)} %bitcast.7, bf16[384,1792]{1,0:T(8,128)(2,1)S(1)} %bitcast.6), custom_call_target="tpu_custom_call" | custom-call | flops 352321536 | bytes 2293760 | tf_op jit(solution)/shard_map/finish/pallas_call | solution.py:346
  (52 shorter events, 0.4 us)
Async XLA Ops:
  0.0 2.8 %collective-permute-start.1 = (bf16[64,7168]{1,0:T(8,128)(2,1)}, bf16[64,7168]{1,0:T(8,128)(2,1)S(1)}, u32[]{:S(2)}, u32[]{:S(2)}) collective-permute-start(bf16[64,7168]{1,0:T(8,128)(2,1)} %own_ref.1), channel_id=1, source_target_pairs={{0,8},{8,0},{1,9},{9,1},{2,10},{10,2},{3,11},{11,3},{4,12},{12,4},... | collective-permute-start | bytes 2752520 | tf_op jit(solution)/shard_map/ppermute | solution.py:382
  1.1 1.4 %collective-permute-start = (s32[1,64]{1,0:T(1,128)S(1)}, s32[1,64]{1,0:T(1,128)S(1)}, u32[]{:S(2)}, u32[]{:S(2)}) collective-permute-start(s32[1,64]{1,0:T(1,128)S(1)} %add_bitcast_fusion.own_pick), channel_id=1, source_target_pairs={{0,8},{8,0},{1,9},{9,1},{2,10},{10,2},{3,11},{11,3},{4,12},{12,4},... | collective-permute-start | bytes 776 | tf_op jit(solution)/shard_map/ppermute | solution.py:382
  7.2 11.7 %collective-permute-start.2 = (bf16[48,896]{1,0:T(8,128)(2,1)}, bf16[48,896]{1,0:T(8,128)(2,1)S(1)}, u32[]{:S(2)}, u32[]{:S(2)}) collective-permute-start(bf16[48,896]{1,0:T(8,128)(2,1)} %get-tuple-element.34), channel_id=1, source_target_pairs={{0,6},{1,7},{2,4},{3,5},{4,2},{5,3},{6,0},{7,1},{8,14},{9,15},{10,... | collective-permute-start | bytes 258056 | tf_op jit(solution)/shard_map/ppermute | solution.py:377
  12.1 11.4 %collective-permute-start.4 = (bf16[48,896]{1,0:T(8,128)(2,1)}, bf16[48,896]{1,0:T(8,128)(2,1)S(1)}, u32[]{:S(2)}, u32[]{:S(2)}) collective-permute-start(bf16[48,896]{1,0:T(8,128)(2,1)} %get-tuple-element.37), channel_id=1, source_target_pairs={{0,5},{1,4},{2,7},{3,6},{4,1},{5,0},{6,3},{7,2},{8,13},{9,12},{10,... | collective-permute-start | bytes 258056 | tf_op jit(solution)/shard_map/ppermute | solution.py:377
  12.5 11.0 %collective-permute-start.6 = (bf16[48,896]{1,0:T(8,128)(2,1)}, bf16[48,896]{1,0:T(8,128)(2,1)S(1)}, u32[]{:S(2)}, u32[]{:S(2)}) collective-permute-start(bf16[48,896]{1,0:T(8,128)(2,1)} %get-tuple-element.40), channel_id=1, source_target_pairs={{0,3},{1,2},{2,1},{3,0},{4,7},{5,6},{6,5},{7,4},{8,11},{9,10},{10,... | collective-permute-start | bytes 258056 | tf_op jit(solution)/shard_map/ppermute | solution.py:377
  13.7 9.9 %collective-permute-start.8 = (bf16[48,896]{1,0:T(8,128)(2,1)}, bf16[48,896]{1,0:T(8,128)(2,1)S(1)}, u32[]{:S(2)}, u32[]{:S(2)}) collective-permute-start(bf16[48,896]{1,0:T(8,128)(2,1)} %get-tuple-element.43), channel_id=1, source_target_pairs={{0,7},{1,6},{2,5},{3,4},{4,3},{5,2},{6,1},{7,0},{8,15},{9,14},{10,... | collective-permute-start | bytes 258056 | tf_op jit(solution)/shard_map/ppermute | solution.py:377
  18.3 8.1 %collective-permute-start.13 = (bf16[48,896]{1,0:T(8,128)(2,1)}, bf16[48,896]{1,0:T(8,128)(2,1)S(1)}, u32[]{:S(2)}, u32[]{:S(2)}) collective-permute-start(bf16[48,896]{1,0:T(8,128)(2,1)} %get-tuple-element.52), channel_id=1, source_target_pairs={{0,1},{1,0},{2,3},{3,2},{4,5},{5,4},{6,7},{7,6},{8,9},{9,8},{10,11... | collective-permute-start | bytes 258056 | tf_op jit(solution)/shard_map/ppermute | solution.py:377
  18.9 15.8 %copy-start.2 = (bf16[48,896]{1,0:T(8,128)(2,1)}, bf16[48,896]{1,0:T(8,128)(2,1)S(1)}, u32[]{:S(2)}) copy-start(bf16[48,896]{1,0:T(8,128)(2,1)S(1)} %collective-permute-done.2.refs_6_) | copy-start | bytes 258052
  18.9 9.0 %collective-permute-start.14 = (bf16[48,896]{1,0:T(8,128)(2,1)}, bf16[48,896]{1,0:T(8,128)(2,1)S(1)}, u32[]{:S(2)}, u32[]{:S(2)}) collective-permute-start(bf16[48,896]{1,0:T(8,128)(2,1)} %get-tuple-element.53), channel_id=1, source_target_pairs={{0,2},{1,3},{2,0},{3,1},{4,6},{5,7},{6,4},{7,5},{8,10},{9,11},{10,... | collective-permute-start | bytes 258056 | tf_op jit(solution)/shard_map/ppermute | solution.py:377
  23.5 11.2 %copy-start.3 = (bf16[48,896]{1,0:T(8,128)(2,1)}, bf16[48,896]{1,0:T(8,128)(2,1)S(1)}, u32[]{:S(2)}) copy-start(bf16[48,896]{1,0:T(8,128)(2,1)S(1)} %collective-permute-done.4.refs_5_) | copy-start | bytes 258052
  23.5 7.7 %collective-permute-start.15 = (bf16[48,896]{1,0:T(8,128)(2,1)}, bf16[48,896]{1,0:T(8,128)(2,1)S(1)}, u32[]{:S(2)}, u32[]{:S(2)}) collective-permute-start(bf16[48,896]{1,0:T(8,128)(2,1)} %get-tuple-element.54), channel_id=1, source_target_pairs={{0,4},{1,5},{2,6},{3,7},{4,0},{5,1},{6,2},{7,3},{8,12},{9,13},{10,... | collective-permute-start | bytes 258056 | tf_op jit(solution)/shard_map/ppermute | solution.py:377
  23.5 11.2 %copy-start.4 = (bf16[48,896]{1,0:T(8,128)(2,1)}, bf16[48,896]{1,0:T(8,128)(2,1)S(1)}, u32[]{:S(2)}) copy-start(bf16[48,896]{1,0:T(8,128)(2,1)S(1)} %collective-permute-done.6.refs_3_) | copy-start | bytes 258052
  23.5 8.5 %collective-permute-start.3 = (bf16[48,896]{1,0:T(8,128)(2,1)}, bf16[48,896]{1,0:T(8,128)(2,1)S(1)}, u32[]{:S(2)}, u32[]{:S(2)}) collective-permute-start(bf16[48,896]{1,0:T(8,128)(2,1)} %get-tuple-element.35), channel_id=1, source_target_pairs={{0,1},{1,0},{2,3},{3,2},{4,5},{5,4},{6,7},{7,6},{8,9},{9,8},{10,11... | collective-permute-start | bytes 258056 | tf_op jit(solution)/shard_map/ppermute | solution.py:377
  23.6 11.1 %copy-start.6 = (bf16[48,896]{1,0:T(8,128)(2,1)}, bf16[48,896]{1,0:T(8,128)(2,1)S(1)}, u32[]{:S(2)}) copy-start(bf16[48,896]{1,0:T(8,128)(2,1)S(1)} %collective-permute-done.8.refs_7_) | copy-start | bytes 258052
  23.6 11.1 %collective-permute-start.5 = (bf16[48,896]{1,0:T(8,128)(2,1)}, bf16[48,896]{1,0:T(8,128)(2,1)S(1)}, u32[]{:S(2)}, u32[]{:S(2)}) collective-permute-start(bf16[48,896]{1,0:T(8,128)(2,1)} %get-tuple-element.38), channel_id=1, source_target_pairs={{0,2},{1,3},{2,0},{3,1},{4,6},{5,7},{6,4},{7,5},{8,10},{9,11},{10,... | collective-permute-start | bytes 258056 | tf_op jit(solution)/shard_map/ppermute | solution.py:377
  26.4 20.7 %collective-permute-start.7 = (bf16[48,896]{1,0:T(8,128)(2,1)}, bf16[48,896]{1,0:T(8,128)(2,1)S(1)}, u32[]{:S(2)}, u32[]{:S(2)}) collective-permute-start(bf16[48,896]{1,0:T(8,128)(2,1)} %get-tuple-element.41), channel_id=1, source_target_pairs={{0,3},{1,2},{2,1},{3,0},{4,7},{5,6},{6,5},{7,4},{8,11},{9,10},{10,... | collective-permute-start | bytes 258056 | tf_op jit(solution)/shard_map/ppermute | solution.py:377
  27.9 19.2 %collective-permute-start.10 = (bf16[48,896]{1,0:T(8,128)(2,1)}, bf16[48,896]{1,0:T(8,128)(2,1)S(1)}, u32[]{:S(2)}, u32[]{:S(2)}) collective-permute-start(bf16[48,896]{1,0:T(8,128)(2,1)} %get-tuple-element.46), channel_id=1, source_target_pairs={{0,5},{1,4},{2,7},{3,6},{4,1},{5,0},{6,3},{7,2},{8,13},{9,12},{10,... | collective-permute-start | bytes 258056 | tf_op jit(solution)/shard_map/ppermute | solution.py:377
  31.2 16.0 %collective-permute-start.11 = (bf16[48,896]{1,0:T(8,128)(2,1)}, bf16[48,896]{1,0:T(8,128)(2,1)S(1)}, u32[]{:S(2)}, u32[]{:S(2)}) collective-permute-start(bf16[48,896]{1,0:T(8,128)(2,1)} %get-tuple-element.48), channel_id=1, source_target_pairs={{0,6},{1,7},{2,4},{3,5},{4,2},{5,3},{6,0},{7,1},{8,14},{9,15},{10,... | collective-permute-start | bytes 258056 | tf_op jit(solution)/shard_map/ppermute | solution.py:377
  32.0 15.0 %copy-start.5 = (bf16[48,896]{1,0:T(8,128)(2,1)}, bf16[48,896]{1,0:T(8,128)(2,1)S(1)}, u32[]{:S(2)}) copy-start(bf16[48,896]{1,0:T(8,128)(2,1)S(1)} %collective-permute-done.3.refs_1_) | copy-start | bytes 258052
  32.0 15.1 %collective-permute-start.12 = (bf16[48,896]{1,0:T(8,128)(2,1)}, bf16[48,896]{1,0:T(8,128)(2,1)S(1)}, u32[]{:S(2)}, u32[]{:S(2)}) collective-permute-start(bf16[48,896]{1,0:T(8,128)(2,1)} %get-tuple-element.50), channel_id=1, source_target_pairs={{0,7},{1,6},{2,5},{3,4},{4,3},{5,2},{6,1},{7,0},{8,15},{9,14},{10,... | collective-permute-start | bytes 258056 | tf_op jit(solution)/shard_map/ppermute | solution.py:377
  34.7 12.4 %copy-start.8 = (bf16[48,896]{1,0:T(8,128)(2,1)}, bf16[48,896]{1,0:T(8,128)(2,1)S(1)}, u32[]{:S(2)}) copy-start(bf16[48,896]{1,0:T(8,128)(2,1)S(1)} %collective-permute-done.5.refs_2_) | copy-start | bytes 258052
  34.7 12.5 %collective-permute-start.9 = (bf16[48,896]{1,0:T(8,128)(2,1)}, bf16[48,896]{1,0:T(8,128)(2,1)S(1)}, u32[]{:S(2)}, u32[]{:S(2)}) collective-permute-start(bf16[48,896]{1,0:T(8,128)(2,1)} %get-tuple-element.44), channel_id=1, source_target_pairs={{0,4},{1,5},{2,6},{3,7},{4,0},{5,1},{6,2},{7,3},{8,12},{9,13},{10,... | collective-permute-start | bytes 258056 | tf_op jit(solution)/shard_map/ppermute | solution.py:377
  47.9 62.3 %copy-start = (f32[64,1]{0,1:T(1,128)S(1)}, f32[64,1]{0,1:T(1,128)}, u32[]{:S(2)}) copy-start(f32[64,1]{0,1:T(1,128)} %param.13) | copy-start | bytes 772
  47.9 62.3 %copy-start.1 = (s32[1,64]{1,0:T(1,128)S(1)}, s32[1,64]{1,0:T(1,128)}, u32[]{:S(2)}) copy-start(s32[1,64]{1,0:T(1,128)} %get-tuple-element.31.base_ref) | copy-start | bytes 772
  (11 other events, 25.1 us)

commit v5 on v4

--- a/solution.py
+++ b/solution.py
@@ -2,7 +2,6 @@
 
 import jax
 import jax.numpy as jnp
-import numpy as np
 from jax import lax
 from jax.experimental import pallas as pl
 from jax.experimental.pallas import tpu as pltpu
@@ -18,7 +17,7 @@
 LAG = 3
 DISPATCH = (896, 896)
 BACK_COLUMNS = 512
-VMEM_BYTES = 56 * 1024 * 1024
+VMEM_BYTES = 40 * 1024 * 1024
 
 
 def route_tables(experts, replicas, gates, placement, slot_count, capacity):
@@ -97,23 +96,13 @@
     return pl.CostEstimate(flops=int(flops), bytes_accessed=int(size), transcendentals=0)
 
 
-def fold_matrix(groups):
-    g, q, c = np.meshgrid(np.arange(groups), np.arange(FOLD), np.arange(CAP), indexing="ij")
-    size = groups * FOLD * CAP
-    matrix = np.zeros((size, size), np.float32)
-    matrix[
-        (q * groups * CAP + g * CAP + c).ravel(), (g * FOLD * CAP + q * CAP + c).ravel()
-    ] = 1.0
-    return matrix
-
-
-def fold_table(n_local):
-    q, k, b, c = np.meshgrid(
-        np.arange(FOLD), np.arange(n_local), np.arange(2), np.arange(CAP), indexing="ij"
-    )
-    table = np.zeros((8, q.size), np.int32)
-    table[0], table[1], table[2] = k.ravel(), b.ravel(), (q * CAP + c).ravel()
-    return table
+def unpack_row(row, groups):
+    part = jnp.zeros_like(row)
+    for q in range(1, FOLD):
+        part = part + (row >= q * groups * CAP).astype(jnp.int32)
+    place = row - part * (groups * CAP)
+    group = ((place.astype(jnp.float32) + 0.5) * (1.0 / CAP)).astype(jnp.int32)
+    return group, part * CAP + place - group * CAP
 
 
 def dispatch_kernel(n_local, place_ref, own_pick, mate_pick, own_ref, mate_ref, spot_ref, *blocks):
@@ -206,10 +195,13 @@
         return self.parts[n][...]
 
 
-def unfold(blocks, order_ref, x_ref):
+def unfold(blocks, x_ref):
     rows, width = x_ref.shape[0], blocks[0].shape[1]
+    size = rows * FOLD
+    group, inner = unpack_row(lax.broadcasted_iota(jnp.int32, (size, size), 0), rows // CAP)
+    order = lax.broadcasted_iota(jnp.int32, (size, size), 1) == group * (FOLD * CAP) + inner
     folded = jnp.concatenate([b[...] for b in blocks], axis=0)
-    value = jnp.dot(order_ref[...], folded, preferred_element_type=jnp.float32)
+    value = jnp.dot(order.astype(jnp.bfloat16), folded, preferred_element_type=jnp.float32)
     value = value.astype(jnp.bfloat16)
     for q in range(FOLD):
         x_ref[:, q * width : (q + 1) * width] = value[q * rows : (q + 1) * rows]
@@ -233,15 +225,15 @@
     ]
 
 
-def first_kernel(n_local, start, order_ref, *refs):
+def first_kernel(n_local, start, *refs):
     blocks = refs[:n_local]
     wg_ref, wu_ref, accg_ref, accu_ref, x_ref, w_ref, sem = refs[n_local:]
     tiles = Stream((w_ref, sem, in_tiles(wg_ref, wu_ref, start, x_ref.shape[1] // STEP)))
-    unfold(blocks, order_ref, x_ref)
+    unfold(blocks, x_ref)
     project(x_ref, tiles, (accg_ref, accu_ref), None)
 
 
-def first_part(order, blocks, gate_weight, up_weight, start):
+def first_part(blocks, gate_weight, up_weight, start):
     n_local = len(blocks)
     rows = 2 * n_local * CAP
     model, hidden = FOLD * blocks[0].shape[1], gate_weight.shape[2]
@@ -249,7 +241,7 @@
     return pl.pallas_call(
         functools.partial(first_kernel, n_local, start),
         out_shape=[acc, acc],
-        in_specs=[VMEM] * (1 + n_local) + [HBM] * 2,
+        in_specs=[VMEM] * n_local + [HBM] * 2,
         out_specs=[VMEM, VMEM],
         scratch_shapes=[
             pltpu.VMEM((rows, model), jnp.bfloat16),
@@ -259,10 +251,10 @@
         compiler_params=params(),
         cost_estimate=cost(4 * rows * model * hidden, 4 * model * hidden),
         name="first_part",
-    )(order, *blocks, gate_weight, up_weight)
-
-
-def second_kernel(n_local, start, order_ref, table_ref, *refs):
+    )(*blocks, gate_weight, up_weight)
+
+
+def second_kernel(n_local, start, *refs):
     blocks, refs = refs[:n_local], refs[n_local:]
     ing_ref, inu_ref, wg_ref, wu_ref, wd_ref, out_ref = refs[:6]
     x_ref, accg_ref, accu_ref, hidden_ref, w_ref, d_ref, sem, dsem = refs[6:]
@@ -274,11 +266,12 @@
         (d_ref, dsem, out_tiles),
     )
     node, local = lax.axis_index("node"), lax.axis_index("local")
-    device = (table_ref[1:2, :] ^ node) * n_local + (table_ref[0:1, :] ^ local)
-    target = device * (FOLD * CAP) + table_ref[2:3, :]
-    size = target.shape[1]
+    size = x_ref.shape[0] * FOLD
+    group, inner = unpack_row(lax.broadcasted_iota(jnp.int32, (size, size), 1), 2 * n_local)
+    device = ((group & 1) ^ node) * n_local + ((group >> 1) ^ local)
+    target = device * (FOLD * CAP) + inner
     back = (lax.broadcasted_iota(jnp.int32, (size, size), 0) == target).astype(jnp.bfloat16)
-    unfold(blocks, order_ref, x_ref)
+    unfold(blocks, x_ref)
     project(x_ref, tiles, (accg_ref, accu_ref), (ing_ref, inu_ref))
     gate_val = accg_ref[...]
     hidden_ref[...] = (gate_val / (1.0 + jnp.exp(-gate_val)) * accu_ref[...]).astype(jnp.bfloat16)
@@ -292,14 +285,14 @@
         ).astype(jnp.bfloat16)
 
 
-def second_part(order, table, blocks, accs, gate_weight, up_weight, down_weight, start):
+def second_part(blocks, accs, gate_weight, up_weight, down_weight, start):
     n_local = len(blocks)
     rows = 2 * n_local * CAP
     model, hidden, whole = FOLD * blocks[0].shape[1], down_weight.shape[1], down_weight.shape[2]
     return pl.pallas_call(
         functools.partial(second_kernel, n_local, start),
         out_shape=jax.ShapeDtypeStruct((rows * FOLD, whole // FOLD), jnp.bfloat16),
-        in_specs=[VMEM] * (4 + n_local) + [HBM] * 3,
+        in_specs=[VMEM] * (2 + n_local) + [HBM] * 3,
         out_specs=VMEM,
         scratch_shapes=[
             pltpu.VMEM((rows, model), jnp.bfloat16),
@@ -316,7 +309,7 @@
             2 * rows * (2 * model + whole) * hidden, 2 * (2 * model + whole) * hidden
         ),
         name="second_part",
-    )(order, table, *blocks, *accs, gate_weight, up_weight, down_weight)
+    )(*blocks, *accs, gate_weight, up_weight, down_weight)
 
 
 def column(row):
@@ -388,16 +381,14 @@
     tok = tokens.shape[0]
     n_local = lax.axis_size("local")
     slots = 2 * n_local
-    order = jnp.asarray(fold_matrix(slots), jnp.bfloat16)
-    table = jnp.asarray(fold_table(n_local))
     mate = swap_mate(tokens)
     pick = (experts * placement.shape[1] + replicas).reshape(1, tok)
     spot, pieces = dispatch(placement, pick, swap_mate(pick), tokens, mate, n_local)
     early = swap_hops(pieces[0])
     late = swap_hops(pieces[1], early)
-    accs = first_part(order, early, gate_weight, up_weight, 0)
+    accs = first_part(early, gate_weight, up_weight, 0)
     start = FOLD * DISPATCH[0]
-    results = second_part(order, table, late, accs, gate_weight, up_weight, down_weight, start)
+    results = second_part(late, accs, gate_weight, up_weight, down_weight, start)
     return finish(spot, gates, [swap(results, slots)])
 
 

time: 113 us -> 106 us (0.938)
  Pallas kernels: 40.4 us -> 34.4 us
    pallas_call x1, Pallas kernels: 22.6 us -> 20.1 us  [second_part(): pl.pallas_call(functools.partial(second_kernel, n_local, start), out_shap...]
    pallas_call x1, Pallas kernels: 12.3 us -> 10.5 us  [first_part(): pl.pallas_call(functools.partial(first_kernel, n_local, start), out_shape...]
    pallas_call x1, Pallas kernels: 3.47 us -> 1.75 us  [dispatch(): pl.pallas_call(functools.partial(dispatch_kernel, n_local), out_shape=out...]
  transfers between devices with their start and end apart: 16 -> 16, of which waited for: 3 -> 3; matrix products, arithmetic and copies ran while one was open for 1% -> 1% of each run, Pallas kernels for 11% -> 10%
where the time goes in v5:
time: 106 us
  blocking collectives  39.7 us (37%)
  Pallas kernels  34.4 us (32%)
  starting transfers between devices  23.4 us (22%)
  waiting for transfers between devices  5.99 us (6%)
  local copies, waits for them, and re-layouts  1.86 us (2%)
    all_to_all x1, blocking collectives, swap(): lax.all_to_all(block.reshape(slots, rows // slots, width), ('node', 'loca...  39.7 us
    ppermute x14, starting transfers between devices, swap_hops(): lax.ppermute(block, 'local', [(i, i ^ hop) for i in range(n_local)])  22.9 us
    pallas_call x1, Pallas kernels, second_part(): pl.pallas_call(functools.partial(second_kernel, n_local, start), out_shap...  20.1 us
    pallas_call x1, Pallas kernels, first_part(): pl.pallas_call(functools.partial(first_kernel, n_local, start), out_shape...  10.5 us
    ppermute x14, waiting for transfers between devices, swap_hops(): lax.ppermute(block, 'local', [(i, i ^ hop) for i in range(n_local)])  4.42 us
  transfers between devices with their start and end apart: 16, of which 3 were waited for; matrix products, arithmetic and copies ran while one was open for 1% of the time, Pallas kernels for 10%

profile of v5, /device:TPU:0, one launch (start us, length us, event | category | flops | bytes accessed | tf_op | source)
XLA Modules:
  0.0 106.2 jit_solution(11519477864881766306)
XLA Ops:
  0.0 0.5 collective-permute-start.1
  0.5 0.7 add_bitcast_fusion.own_pick
  1.1 0.1 collective-permute-start
  1.2 1.4 %collective-permute-done.mate_pick = s32[1,64]{1,0:T(1,128)S(1)} collective-permute-done((s32[1,64]{1,0:T(1,128)S(1)}, s32[1,64]{1,0:T(1,128)S(1)}, u32[]{:S(2)}, u32[]{:S(2)}) %collective-permute-start) | collective-permute-done | bytes 288 | tf_op jit(solution)/shard_map/ppermute | solution.py:375
  2.6 0.2 collective-permute-done.1.mate_ref
  2.8 1.2 %copy-done.1 = bf16[64,7168]{1,0:T(8,128)(2,1)S(1)} copy-done((bf16[64,7168]{1,0:T(8,128)(2,1)S(1)}, bf16[64,7168]{1,0:T(8,128)(2,1)}, u32[]{:S(2)}) %copy-start.1) | copy-done | bytes 917528
  3.9 0.7 copy-done.2
  4.6 1.8 %dispatch.1 = (s32[1,64]{1,0:T(1,128)S(1)}, bf16[48,896]{1,0:T(8,128)(2,1)S(1)}, bf16[48,896]{1,0:T(8,128)(2,1)S(1)}, bf16[48,896]{1,0:T(8,128)(2,1)S(1)}, bf16[...) custom-call(s32[2,12]{1,0:T(2,128)S(1)} %bitcast.9, ...), custom_call_target="tpu_custom_call" | custom-call | flops 704643072 | bytes 4587520 | tf_op jit(solution)/shard_map/dispatch/pallas_call | solution.py:163
  6.4 5.0 %collective-permute-start.2 = (bf16[48,896]{1,0:T(8,128)(2,1)S(1)}, bf16[48,896]{1,0:T(8,128)(2,1)S(1)}, u32[]{:S(2)}, u32[]{:S(2)}) collective-permute-start(bf16[48,896]{1,0:T(8,128)(2,1)S(1)} %get-tuple-element.34), channel_id=1, source_target_pairs={{0,6},{1,7},{2,4},{3,5},{4,2},{5,3},{6,0},{7,1},{8,14},{9,15},{10,... | collective-permute-start | bytes 258056 | tf_op jit(solution)/shard_map/ppermute | solution.py:370
  11.4 0.4 collective-permute-start.4
  11.8 1.2 %collective-permute-start.6 = (bf16[48,896]{1,0:T(8,128)(2,1)S(1)}, bf16[48,896]{1,0:T(8,128)(2,1)S(1)}, u32[]{:S(2)}, u32[]{:S(2)}) collective-permute-start(bf16[48,896]{1,0:T(8,128)(2,1)S(1)} %get-tuple-element.40), channel_id=1, source_target_pairs={{0,3},{1,2},{2,1},{3,0},{4,7},{5,6},{6,5},{7,4},{8,11},{9,10},{10,... | collective-permute-start | bytes 258056 | tf_op jit(solution)/shard_map/ppermute | solution.py:370
  13.0 4.7 %collective-permute-start.8 = (bf16[48,896]{1,0:T(8,128)(2,1)S(1)}, bf16[48,896]{1,0:T(8,128)(2,1)S(1)}, u32[]{:S(2)}, u32[]{:S(2)}) collective-permute-start(bf16[48,896]{1,0:T(8,128)(2,1)S(1)} %get-tuple-element.43), channel_id=1, source_target_pairs={{0,7},{1,6},{2,5},{3,4},{4,3},{5,2},{6,1},{7,0},{8,15},{9,14},{10,... | collective-permute-start | bytes 258056 | tf_op jit(solution)/shard_map/ppermute | solution.py:370
  17.6 0.5 collective-permute-start.13
  18.2 4.4 %collective-permute-done.4.refs_5_ = bf16[48,896]{1,0:T(8,128)(2,1)S(1)} collective-permute-done((bf16[48,896]{1,0:T(8,128)(2,1)S(1)}, bf16[48,896]{1,0:T(8,128)(2,1)S(1)}, u32[]{:S(2)}, u32[]{:S(2)}) %collective-permute-start.4) | collective-permute-done | bytes 86048 | tf_op jit(solution)/shard_map/ppermute | solution.py:370
  22.6 2.8 %collective-permute-start.5 = (bf16[48,896]{1,0:T(8,128)(2,1)S(1)}, bf16[48,896]{1,0:T(8,128)(2,1)S(1)}, u32[]{:S(2)}, u32[]{:S(2)}) collective-permute-start(bf16[48,896]{1,0:T(8,128)(2,1)S(1)} %get-tuple-element.38), channel_id=1, source_target_pairs={{0,2},{1,3},{2,0},{3,1},{4,6},{5,7},{6,4},{7,5},{8,10},{9,11},{10,... | collective-permute-start | bytes 258056 | tf_op jit(solution)/shard_map/ppermute | solution.py:370
  25.4 1.5 %collective-permute-start.7 = (bf16[48,896]{1,0:T(8,128)(2,1)S(1)}, bf16[48,896]{1,0:T(8,128)(2,1)S(1)}, u32[]{:S(2)}, u32[]{:S(2)}) collective-permute-start(bf16[48,896]{1,0:T(8,128)(2,1)S(1)} %get-tuple-element.41), channel_id=1, source_target_pairs={{0,3},{1,2},{2,1},{3,0},{4,7},{5,6},{6,5},{7,4},{8,11},{9,10},{10,... | collective-permute-start | bytes 258056 | tf_op jit(solution)/shard_map/ppermute | solution.py:370
  26.9 3.5 %collective-permute-start.10 = (bf16[48,896]{1,0:T(8,128)(2,1)S(1)}, bf16[48,896]{1,0:T(8,128)(2,1)S(1)}, u32[]{:S(2)}, u32[]{:S(2)}) collective-permute-start(bf16[48,896]{1,0:T(8,128)(2,1)S(1)} %get-tuple-element.46), channel_id=1, source_target_pairs={{0,5},{1,4},{2,7},{3,6},{4,1},{5,0},{6,3},{7,2},{8,13},{9,12},{10,... | collective-permute-start | bytes 258056 | tf_op jit(solution)/shard_map/ppermute | solution.py:370
  30.4 0.3 collective-permute-start.11
  30.7 3.0 %collective-permute-start.12 = (bf16[48,896]{1,0:T(8,128)(2,1)S(1)}, bf16[48,896]{1,0:T(8,128)(2,1)S(1)}, u32[]{:S(2)}, u32[]{:S(2)}) collective-permute-start(bf16[48,896]{1,0:T(8,128)(2,1)S(1)} %get-tuple-element.50), channel_id=1, source_target_pairs={{0,7},{1,6},{2,5},{3,4},{4,3},{5,2},{6,1},{7,0},{8,15},{9,14},{10,... | collective-permute-start | bytes 258056 | tf_op jit(solution)/shard_map/ppermute | solution.py:370
  33.7 10.5 %first_part.1 = (f32[96,2048]{1,0:T(8,128)S(1)}, f32[96,2048]{1,0:T(8,128)S(1)}) custom-call(bf16[48,896]{1,0:T(8,128)(2,1)S(1)} %get-tuple-element.51.refs_0_, bf16[48,896]{1,0:T(8,128)(2,1)S(1)} %collective-permute-done.13.refs_1_, bf16[48,896]{1,0:T(8,128)(2,1)S(1)} %collective-permute-done.14.refs_2_, ...), custom_call_target="tpu_custom_call" | custom-call | flops 2818572288 | bytes 29360128 | tf_op jit(solution)/shard_map/first_part/pallas_call | solution.py:241
  44.3 0.0 copy-start
  44.3 20.1 %second_part.1 = bf16[384,1792]{1,0:T(8,128)(2,1)S(1)} custom-call(bf16[48,896]{1,0:T(8,128)(2,1)S(1)} %get-tuple-element.32.refs_0_, bf16[48,896]{1,0:T(8,128)(2,1)S(1)} %collective-permute-done.3.refs_1_, bf16[48,896]{1,0:T(8,128)(2,1)S(1)} %collective-permute-done.5.refs_2_, bf16[48,896]{1,0:T(8,128)(2,1)S(1)} %collective-permute-done.7.refs_3_, ...), custom_call_target="tpu_custom_call" | custom-call | flops 5637144576 | bytes 58720256 | tf_op jit(solution)/shard_map/second_part/pallas_call | solution.py:292
  64.4 39.7 %all_to_all.5 = bf16[16,24,1792]{2,1,0:T(8,128)(2,1)S(1)} all-to-all(bf16[16,24,1792]{2,1,0:T(8,128)(2,1)S(1)} %bitcast.7), channel_id=1, replica_groups=mesh['parts'=2,'node'=2,'local'=8] {'node','local'}, dimensions={0} | all-to-all | bytes 2752512 | tf_op jit(solution)/shard_map/all_to_all | solution.py:352
  104.1 2.1 %finish.1 = bf16[64,7168]{1,0:T(8,128)(2,1)} custom-call(s32[1,64]{1,0:T(1,128)S(1)} %get-tuple-element.31.base_ref, f32[1,64]{1,0:T(1,128)S(1)} %bitcast.8, bf16[384,1792]{1,0:T(8,128)(2,1)S(1)} %bitcast.6), custom_call_target="tpu_custom_call" | custom-call | flops 352321536 | bytes 2293760 | tf_op jit(solution)/shard_map/finish/pallas_call | solution.py:339
  (20 shorter events, 0.1 us)
Async XLA Ops:
  0.0 2.8 %collective-permute-start.1 = (bf16[64,7168]{1,0:T(8,128)(2,1)}, bf16[64,7168]{1,0:T(8,128)(2,1)S(1)}, u32[]{:S(2)}, u32[]{:S(2)}) collective-permute-start(bf16[64,7168]{1,0:T(8,128)(2,1)} %own_ref.1), channel_id=1, source_target_pairs={{0,8},{8,0},{1,9},{9,1},{2,10},{10,2},{3,11},{11,3},{4,12},{12,4},... | collective-permute-start | bytes 2752520 | tf_op jit(solution)/shard_map/ppermute | solution.py:375
  1.1 1.4 %collective-permute-start = (s32[1,64]{1,0:T(1,128)S(1)}, s32[1,64]{1,0:T(1,128)S(1)}, u32[]{:S(2)}, u32[]{:S(2)}) collective-permute-start(s32[1,64]{1,0:T(1,128)S(1)} %add_bitcast_fusion.own_pick), channel_id=1, source_target_pairs={{0,8},{8,0},{1,9},{9,1},{2,10},{10,2},{3,11},{11,3},{4,12},{12,4},... | collective-permute-start | bytes 776 | tf_op jit(solution)/shard_map/ppermute | solution.py:375
  2.8 1.2 %copy-start.1 = (bf16[64,7168]{1,0:T(8,128)(2,1)S(1)}, bf16[64,7168]{1,0:T(8,128)(2,1)}, u32[]{:S(2)}) copy-start(bf16[64,7168]{1,0:T(8,128)(2,1)} %own_ref.1) | copy-start | bytes 2752516
  3.9 0.7 copy-start.2
  6.4 11.8 %collective-permute-start.2 = (bf16[48,896]{1,0:T(8,128)(2,1)S(1)}, bf16[48,896]{1,0:T(8,128)(2,1)S(1)}, u32[]{:S(2)}, u32[]{:S(2)}) collective-permute-start(bf16[48,896]{1,0:T(8,128)(2,1)S(1)} %get-tuple-element.34), channel_id=1, source_target_pairs={{0,6},{1,7},{2,4},{3,5},{4,2},{5,3},{6,0},{7,1},{8,14},{9,15},{10,... | collective-permute-start | bytes 258056 | tf_op jit(solution)/shard_map/ppermute | solution.py:370
  11.4 11.1 %collective-permute-start.4 = (bf16[48,896]{1,0:T(8,128)(2,1)S(1)}, bf16[48,896]{1,0:T(8,128)(2,1)S(1)}, u32[]{:S(2)}, u32[]{:S(2)}) collective-permute-start(bf16[48,896]{1,0:T(8,128)(2,1)S(1)} %get-tuple-element.37), channel_id=1, source_target_pairs={{0,5},{1,4},{2,7},{3,6},{4,1},{5,0},{6,3},{7,2},{8,13},{9,12},{10,... | collective-permute-start | bytes 258056 | tf_op jit(solution)/shard_map/ppermute | solution.py:370
  11.8 10.8 %collective-permute-start.6 = (bf16[48,896]{1,0:T(8,128)(2,1)S(1)}, bf16[48,896]{1,0:T(8,128)(2,1)S(1)}, u32[]{:S(2)}, u32[]{:S(2)}) collective-permute-start(bf16[48,896]{1,0:T(8,128)(2,1)S(1)} %get-tuple-element.40), channel_id=1, source_target_pairs={{0,3},{1,2},{2,1},{3,0},{4,7},{5,6},{6,5},{7,4},{8,11},{9,10},{10,... | collective-permute-start | bytes 258056 | tf_op jit(solution)/shard_map/ppermute | solution.py:370
  13.0 9.6 %collective-permute-start.8 = (bf16[48,896]{1,0:T(8,128)(2,1)S(1)}, bf16[48,896]{1,0:T(8,128)(2,1)S(1)}, u32[]{:S(2)}, u32[]{:S(2)}) collective-permute-start(bf16[48,896]{1,0:T(8,128)(2,1)S(1)} %get-tuple-element.43), channel_id=1, source_target_pairs={{0,7},{1,6},{2,5},{3,4},{4,3},{5,2},{6,1},{7,0},{8,15},{9,14},{10,... | collective-permute-start | bytes 258056 | tf_op jit(solution)/shard_map/ppermute | solution.py:370
  17.6 7.8 %collective-permute-start.13 = (bf16[48,896]{1,0:T(8,128)(2,1)S(1)}, bf16[48,896]{1,0:T(8,128)(2,1)S(1)}, u32[]{:S(2)}, u32[]{:S(2)}) collective-permute-start(bf16[48,896]{1,0:T(8,128)(2,1)S(1)} %get-tuple-element.52), channel_id=1, source_target_pairs={{0,1},{1,0},{2,3},{3,2},{4,5},{5,4},{6,7},{7,6},{8,9},{9,8},{10,11... | collective-permute-start | bytes 258056 | tf_op jit(solution)/shard_map/ppermute | solution.py:370
  18.2 8.7 %collective-permute-start.14 = (bf16[48,896]{1,0:T(8,128)(2,1)S(1)}, bf16[48,896]{1,0:T(8,128)(2,1)S(1)}, u32[]{:S(2)}, u32[]{:S(2)}) collective-permute-start(bf16[48,896]{1,0:T(8,128)(2,1)S(1)} %get-tuple-element.53), channel_id=1, source_target_pairs={{0,2},{1,3},{2,0},{3,1},{4,6},{5,7},{6,4},{7,5},{8,10},{9,11},{10,... | collective-permute-start | bytes 258056 | tf_op jit(solution)/shard_map/ppermute | solution.py:370
  22.6 7.9 %collective-permute-start.15 = (bf16[48,896]{1,0:T(8,128)(2,1)S(1)}, bf16[48,896]{1,0:T(8,128)(2,1)S(1)}, u32[]{:S(2)}, u32[]{:S(2)}) collective-permute-start(bf16[48,896]{1,0:T(8,128)(2,1)S(1)} %get-tuple-element.54), channel_id=1, source_target_pairs={{0,4},{1,5},{2,6},{3,7},{4,0},{5,1},{6,2},{7,3},{8,12},{9,13},{10,... | collective-permute-start | bytes 258056 | tf_op jit(solution)/shard_map/ppermute | solution.py:370
  22.6 8.1 %collective-permute-start.3 = (bf16[48,896]{1,0:T(8,128)(2,1)S(1)}, bf16[48,896]{1,0:T(8,128)(2,1)S(1)}, u32[]{:S(2)}, u32[]{:S(2)}) collective-permute-start(bf16[48,896]{1,0:T(8,128)(2,1)S(1)} %get-tuple-element.35), channel_id=1, source_target_pairs={{0,1},{1,0},{2,3},{3,2},{4,5},{5,4},{6,7},{7,6},{8,9},{9,8},{10,11... | collective-permute-start | bytes 258056 | tf_op jit(solution)/shard_map/ppermute | solution.py:370
  22.6 11.1 %collective-permute-start.5 = (bf16[48,896]{1,0:T(8,128)(2,1)S(1)}, bf16[48,896]{1,0:T(8,128)(2,1)S(1)}, u32[]{:S(2)}, u32[]{:S(2)}) collective-permute-start(bf16[48,896]{1,0:T(8,128)(2,1)S(1)} %get-tuple-element.38), channel_id=1, source_target_pairs={{0,2},{1,3},{2,0},{3,1},{4,6},{5,7},{6,4},{7,5},{8,10},{9,11},{10,... | collective-permute-start | bytes 258056 | tf_op jit(solution)/shard_map/ppermute | solution.py:370
  25.4 18.8 %collective-permute-start.7 = (bf16[48,896]{1,0:T(8,128)(2,1)S(1)}, bf16[48,896]{1,0:T(8,128)(2,1)S(1)}, u32[]{:S(2)}, u32[]{:S(2)}) collective-permute-start(bf16[48,896]{1,0:T(8,128)(2,1)S(1)} %get-tuple-element.41), channel_id=1, source_target_pairs={{0,3},{1,2},{2,1},{3,0},{4,7},{5,6},{6,5},{7,4},{8,11},{9,10},{10,... | collective-permute-start | bytes 258056 | tf_op jit(solution)/shard_map/ppermute | solution.py:370
  26.9 17.4 %collective-permute-start.10 = (bf16[48,896]{1,0:T(8,128)(2,1)S(1)}, bf16[48,896]{1,0:T(8,128)(2,1)S(1)}, u32[]{:S(2)}, u32[]{:S(2)}) collective-permute-start(bf16[48,896]{1,0:T(8,128)(2,1)S(1)} %get-tuple-element.46), channel_id=1, source_target_pairs={{0,5},{1,4},{2,7},{3,6},{4,1},{5,0},{6,3},{7,2},{8,13},{9,12},{10,... | collective-permute-start | bytes 258056 | tf_op jit(solution)/shard_map/ppermute | solution.py:370
  30.4 13.8 %collective-permute-start.11 = (bf16[48,896]{1,0:T(8,128)(2,1)S(1)}, bf16[48,896]{1,0:T(8,128)(2,1)S(1)}, u32[]{:S(2)}, u32[]{:S(2)}) collective-permute-start(bf16[48,896]{1,0:T(8,128)(2,1)S(1)} %get-tuple-element.48), channel_id=1, source_target_pairs={{0,6},{1,7},{2,4},{3,5},{4,2},{5,3},{6,0},{7,1},{8,14},{9,15},{10,... | collective-permute-start | bytes 258056 | tf_op jit(solution)/shard_map/ppermute | solution.py:370
  30.7 13.5 %collective-permute-start.12 = (bf16[48,896]{1,0:T(8,128)(2,1)S(1)}, bf16[48,896]{1,0:T(8,128)(2,1)S(1)}, u32[]{:S(2)}, u32[]{:S(2)}) collective-permute-start(bf16[48,896]{1,0:T(8,128)(2,1)S(1)} %get-tuple-element.50), channel_id=1, source_target_pairs={{0,7},{1,6},{2,5},{3,4},{4,3},{5,2},{6,1},{7,0},{8,15},{9,14},{10,... | collective-permute-start | bytes 258056 | tf_op jit(solution)/shard_map/ppermute | solution.py:370
  33.7 10.5 %collective-permute-start.9 = (bf16[48,896]{1,0:T(8,128)(2,1)S(1)}, bf16[48,896]{1,0:T(8,128)(2,1)S(1)}, u32[]{:S(2)}, u32[]{:S(2)}) collective-permute-start(bf16[48,896]{1,0:T(8,128)(2,1)S(1)} %get-tuple-element.44), channel_id=1, source_target_pairs={{0,4},{1,5},{2,6},{3,7},{4,0},{5,1},{6,2},{7,3},{8,12},{9,13},{10,... | collective-permute-start | bytes 258056 | tf_op jit(solution)/shard_map/ppermute | solution.py:370
  44.3 59.8 %copy-start = (f32[64,1]{0,1:T(1,128)S(1)}, f32[64,1]{0,1:T(1,128)}, u32[]{:S(2)}) copy-start(f32[64,1]{0,1:T(1,128)} %param.11) | copy-start | bytes 772
